TPU v7x, 32 devices: a whole 2x2x4 slice. The times are simulated.
32 devices in a mesh: dp: 8 (over z, y), fsdp: 4 (over x, core).
Axes of the slice: x: 2, y: 2, z: 4, core: 2. Of those that a mesh axis runs over, the one named last changes fastest.
Arguments:
- features: bfloat16 [6144, 8192], P(('dp', 'fsdp')), may hold values from -6 to 6
- grad_out: bfloat16 [6144, 8192], P(('dp', 'fsdp')), may hold values from -6 to 6
- weight_tiles: bfloat16 [256, 128, 128], P('fsdp'), may hold values from -0.25 to 0.25
- tile_row: int32 [256], replicated, may hold values from 0 to 63, as said below
- tile_column: int32 [256], replicated, may hold values from 0 to 63, as said below
Outputs:
- grad_features: bfloat16 [6144, 8192], P(('dp', 'fsdp'))
- tile_update: float32 [256, 128, 128], P('fsdp')
Inputs may be any that keep to these rules, and one draw needn't show every extreme that they name: `tile_row`: every tile-row holds exactly 4 stored tiles; the tile-columns of tile-row i are i XOR s for the four values s in (0, 2^a, 2^b, 2^a + 2^b), with two distinct bits a, b drawn per run; the stored order is a random permutation of the pattern. Every tile-column holds exactly 4 stored tiles; no (tile_row, tile_column) pair appears twice.
All inputs are finite; a program needn't handle non-finite values.
Results may differ from a plain program's by a relative error of at most 0.0034.
Values may be sent and summed in bfloat16 or wider, within the bound.
A program may use at most 128 MiB of HBM per device.

v0:
```python
import math

import jax
import jax.numpy as jnp
from jax import lax
from jax.sharding import PartitionSpec as P


def gelu_slope(value):
    root_term = math.sqrt(2.0 / math.pi)
    inner = root_term * (value + 0.044715 * value * value * value)
    hyper = jnp.tanh(inner)
    return 0.5 * (1.0 + hyper) + 0.5 * value * (1.0 - hyper * hyper) * root_term * (
        1.0 + 3.0 * 0.044715 * value * value
    )


def on_device(features, grad_out, weight_tiles, tile_row, tile_column):
    rows_here = features.shape[0]
    side = weight_tiles.shape[1]
    nblocks = features.shape[1] // side
    total_tiles = tile_row.shape[0]
    per_block = total_tiles // nblocks
    feature_blocks = features.reshape(rows_here, nblocks, side)
    grad_blocks = grad_out.reshape(rows_here, nblocks, side)
    order_rows = jnp.argsort(tile_row, stable=True)
    order_columns = jnp.argsort(tile_column, stable=True)
    columns_by_row = tile_column[order_rows].reshape(nblocks, per_block)
    rows_by_column = tile_row[order_columns].reshape(nblocks, per_block)
    whole = lax.all_gather(weight_tiles, "fsdp", axis=0, tiled=True)
    tiles_by_row = whole[order_rows].reshape(nblocks, per_block, side, side)
    taken = feature_blocks[:, columns_by_row]
    preact = jnp.einsum("rnkc,nkcd->rnd", taken, tiles_by_row, preferred_element_type=jnp.float32)
    slope_grad = (grad_blocks.astype(jnp.float32) * gelu_slope(preact)).astype(jnp.bfloat16)
    tiles_by_column = whole[order_columns].reshape(nblocks, per_block, side, side)
    slopes_taken = slope_grad[:, rows_by_column]
    returned = jnp.einsum(
        "rnkd,nkcd->rnc", slopes_taken, tiles_by_column, preferred_element_type=jnp.float32
    )
    grad_features = (
        (grad_blocks.astype(jnp.float32) + returned)
        .astype(jnp.bfloat16)
        .reshape(rows_here, nblocks * side)
    )
    tile_ids = jnp.arange(
        total_tiles // lax.axis_size("fsdp") * lax.axis_size("fsdp"), dtype=jnp.int32
    )
    columns = tile_column[tile_ids]
    row_ids = tile_row[tile_ids]
    picked = jnp.take(feature_blocks, columns, axis=1)
    slopes = jnp.take(slope_grad, row_ids, axis=1)
    summed = lax.psum_scatter(
        jnp.einsum("rnc,rnd->ncd", picked, slopes, preferred_element_type=jnp.float32),
        "fsdp",
        scatter_dimension=0,
        tiled=True,
    )
    weight_grad = lax.psum(summed, "dp")
    tile_update = weight_grad * lax.rsqrt(
        jnp.mean(weight_grad * weight_grad, axis=(1, 2), keepdims=True) + 1e-06
    )
    return (grad_features, tile_update)


def solution(mesh):
    return jax.shard_map(
        on_device,
        mesh=mesh,
        in_specs=(
            P(("dp", "fsdp"), None),
            P(("dp", "fsdp"), None),
            P("fsdp", None, None),
            P(),
            P(),
        ),
        out_specs=(P(("dp", "fsdp"), None), P("fsdp", None, None)),
        check_vma=False,
    )
```

profile of v0, /device:TPU:0, one launch (start us, length us, event | category | flops | bytes accessed | tf_op | source)
XLA Modules:
  0.0 418.2 jit_solution(10438402132896641660)
XLA Ops:
  7.2 0.0 all-gather.2.cloned.1.call-start
  7.2 0.7 all-gather.2.cloned.1.call-update
  7.9 0.0 reduce-scatter.2.cloned.1.call-start
  8.0 4.0 sort.32
  12.0 2.0 gather_fusion.7
  13.9 2.0 gather_fusion.6
  16.0 2.0 gather_fusion.2
  17.9 0.1 reshape.97
  18.1 0.1 reshape.143
  18.2 2.6 copy_bitcast_fusion.1
  20.7 13.2 %gather_fusion.3 = bf16[256,192,128]{2,1,0:T(8,128)(2,1)} fusion(bf16[192,64,128]{2,0,1:T(8,128)(2,1)} %copy_bitcast_fusion.1, s32[1024]{0:T(1024)S(1)} %pad_clamp_fusion.4), kind=kCustom, calls=%fused_computation.5 | custom fusion | bytes 25166848 | tf_op jit(solution)/shard_map/gather | solution.py:32
  34.0 10.7 %gather_fusion.8 = bf16[256,192,128]{2,1,0:T(8,128)(2,1)} fusion(bf16[192,64,128]{2,0,1:T(8,128)(2,1)S(1)} %copy-done.4, s32[1024]{0:T(1024)S(1)} %pad_clamp_fusion.1), kind=kCustom, calls=%fused_computation.clone | custom fusion | bytes 25166848 | tf_op jit(solution)/shard_map/jit(_take)/gather | solution.py:50
  44.7 25.9 %all-gather.2.cloned.1.call-done = bf16[256,128,128]{2,1,0:T(8,128)(2,1)} async-done(((bf16[64,128,128]{2,1,0:T(8,128)(2,1)}), bf16[256,128,128]{2,1,0:T(8,128)(2,1)}) %all-gather.2.cloned.1.call-update) | async-done | bytes 8388624 | tf_op jit(solution)/shard_map/all_gather | solution.py:30
  70.6 12.1 %gather_fusion.1 = bf16[256,128,128]{2,1,0:T(8,128)(2,1)} fusion(bf16[256,128,128]{2,1,0:T(8,128)(2,1)} %all-gather.2.cloned.1.call-done, s32[1024]{0:T(1024)S(1)} %pad_clamp_fusion.5), kind=kCustom, calls=%fused_computation.3 | custom fusion | bytes 16778240 | tf_op jit(solution)/shard_map/gather | solution.py:31
  82.7 11.0 %fusion.13 = bf16[192,64,128]{2,0,1:T(8,128)(2,1)S(1)} fusion(bf16[192,64,4,128]{3,0,2,1:T(8,128)(2,1)} %bitcast.65, bf16[64,4,128,128]{3,2,1,0:T(8,128)(2,1)} %bitcast.68, bf16[192,8192]{1,0:T(8,128)(2,1)} %param.8), kind=kOutput, calls=%fused_computation.25 | convolution fusion | flops 1642070016 | bytes 27262976 | tf_op jit(solution)/shard_map/rnkc,nkcd->rnd/dot_general | solution.py:33
  93.7 10.7 %gather_fusion.9 = bf16[256,192,128]{2,1,0:T(8,128)(2,1)} fusion(bf16[192,64,128]{2,0,1:T(8,128)(2,1)S(1)} %fusion.13, s32[1024]{0:T(1024)S(1)} %pad_clamp_fusion), kind=kCustom, calls=%fused_computation.1.clone | custom fusion | bytes 25166848 | tf_op jit(solution)/shard_map/jit(_take)/gather | solution.py:51
  104.5 14.6 %fusion = f32[256,128,128]{2,1,0:T(8,128)} fusion(bf16[256,192,128]{2,1,0:T(8,128)(2,1)} %gather_fusion.9, bf16[256,192,128]{2,1,0:T(8,128)(2,1)} %gather_fusion.8, pred[256]{0:T(512)(128)(4,1)S(1)} %get-tuple-element.7, pred[256]{0:T(512)(128)(4,1)S(1)} %get-tuple-element.8), kind=kOutput, calls=%fused_computation.10 | convolution fusion | flops 1623195648 | bytes 41943552 | tf_op jit(solution)/shard_map/rnc,rnd->ncd/dot_general | solution.py:53
  119.1 0.0 reduce-scatter.2.cloned.1.call-update
  119.1 0.0 all-reduce.2.cloned.1.call-start
  119.2 126.2 %reduce-scatter.2.cloned.1.call-done = f32[64,128,128]{2,1,0:T(8,128)} async-done(((f32[256,128,128]{2,1,0:T(8,128)}), f32[64,128,128]{2,1,0:T(8,128)}) %reduce-scatter.2.cloned.1.call-update) | async-done | bytes 4194320 | tf_op jit(solution)/shard_map/reduce_scatter | solution.py:52
  245.5 3.2 sort.31
  248.6 2.2 gather_fusion.4
  250.9 0.1 reshape.98
  251.0 0.1 reshape.159
  251.1 12.5 %gather_fusion.5 = bf16[256,192,128]{2,1,0:T(8,128)(2,1)} fusion(bf16[192,64,128]{2,0,1:T(8,128)(2,1)} %copy-done.5, s32[1024]{0:T(1024)S(1)} %pad_clamp_fusion.3), kind=kCustom, calls=%fused_computation.7 | custom fusion | bytes 25166848 | tf_op jit(solution)/shard_map/gather | solution.py:36
  263.6 12.0 %gather_fusion = bf16[256,128,128]{2,1,0:T(8,128)(2,1)} fusion(bf16[256,128,128]{2,1,0:T(8,128)(2,1)} %all-gather.2.cloned.1.call-done, s32[1024]{0:T(1024)S(1)} %pad_clamp_fusion.6), kind=kCustom, calls=%fused_computation.2 | custom fusion | bytes 16778240 | tf_op jit(solution)/shard_map/gather | solution.py:35
  275.7 12.4 %fusion.18 = bf16[64,24,8,128]{3,2,1,0:T(8,128)(2,1)} fusion(bf16[64,4,128,128]{3,2,1,0:T(8,128)(2,1)} %bitcast.67, bf16[192,64,4,128]{3,0,2,1:T(8,128)(2,1)} %bitcast.66, bf16[192,8192]{1,0:T(8,128)(2,1)} %param.8), kind=kOutput, calls=%fused_computation.34 | convolution fusion | flops 1615331328 | bytes 27262976 | tf_op jit(solution)/shard_map/rnkd,nkcd->rnc/dot_general | solution.py:37
  288.1 4.6 %copy.32 = bf16[64,24,8,128]{3,2,0,1:T(8,128)(2,1)} copy(bf16[64,24,8,128]{3,2,1,0:T(8,128)(2,1)} %fusion.18) | data formatting | bytes 6291456 | tf_op jit(solution)/shard_map/reshape | solution.py:43
  292.7 113.2 %all-reduce.2.cloned.1.call-done = f32[64,128,128]{2,1,0:T(8,128)} async-done(((f32[64,128,128]{2,1,0:T(8,128)}), f32[64,128,128]{2,1,0:T(8,128)}) %all-reduce.2.cloned.1.call-update) | async-done | bytes 4194320 | tf_op jit(solution)/shard_map/psum | solution.py:58
  405.9 2.9 multiply_reduce_fusion
  408.8 0.5 copy-done.6
  409.3 2.4 broadcast_multiply_fusion
  (32 shorter events, 0.2 us)
Async XLA Ops:
  7.2 11.0 %copy-start = (bf16[192,8192]{1,0:T(8,128)(2,1)S(1)}, bf16[192,8192]{1,0:T(8,128)(2,1)}, u32[]{:S(2)}) copy-start(bf16[192,8192]{1,0:T(8,128)(2,1)} %param.7) | copy-start | bytes 9437188
  7.2 63.4 %all-gather.2.cloned.1.call-start = ((), (), s32[]{:S(2)}) async-start(), calls=%async_computation.1 | async-start | bytes 10485760 | tf_op jit(solution)/shard_map/all_gather | solution.py:30
  7.9 237.5 %reduce-scatter.2.cloned.1.call-start = ((), (), s32[]{:S(2)}) async-start(), calls=%async_computation.2 | async-start | bytes 20971520 | tf_op jit(solution)/shard_map/reduce_scatter | solution.py:52
  20.7 13.2 %copy-start.4 = (bf16[192,64,128]{2,0,1:T(8,128)(2,1)S(1)}, bf16[192,64,128]{2,0,1:T(8,128)(2,1)}, u32[]{:S(2)}) copy-start(bf16[192,64,128]{2,0,1:T(8,128)(2,1)} %copy_bitcast_fusion.1) | copy-start | bytes 9437188
  93.7 10.7 %copy-start.5 = (bf16[192,64,128]{2,0,1:T(8,128)(2,1)}, bf16[192,64,128]{2,0,1:T(8,128)(2,1)S(1)}, u32[]{:S(2)}) copy-start(bf16[192,64,128]{2,0,1:T(8,128)(2,1)S(1)} %fusion.13) | copy-start | bytes 9437188
  119.1 126.3 %copy-start.2 = (s32[256]{0:T(256)S(1)}, s32[256]{0:T(256)}, u32[]{:S(2)}) copy-start(s32[256]{0:T(256)} %param.11) | copy-start | bytes 3076
  119.1 129.5 %copy-start.3 = (s32[256]{0:T(256)S(1)}, s32[256]{0:T(256)}, u32[]{:S(2)}) copy-start(s32[256]{0:T(256)} %param.10) | copy-start | bytes 3076
  119.1 286.8 %all-reduce.2.cloned.1.call-start = ((), (), s32[]{:S(2)}) async-start(), calls=%async_computation.3 | async-start | bytes 8388608 | tf_op jit(solution)/shard_map/psum | solution.py:58
  288.1 123.6 %copy-start.1 = (bf16[192,8192]{1,0:T(8,128)(2,1)S(1)}, bf16[192,8192]{1,0:T(8,128)(2,1)}, u32[]{:S(2)}) copy-start(bf16[192,8192]{1,0:T(8,128)(2,1)} %param.7) | copy-start | bytes 9437188
  405.9 3.4 copy-start.6
Sparse Core Ops, SparseCore 0:
  9.6 61.0 all-gather.1
  119.2 126.1 reduce-scatter.1
  249.5 156.2 all-reduce.1
where the time goes:
time: 419 us; the launch traced here: 418 us
  waiting for transfers between devices  266 us (63%)
  local copies, waits for them, and re-layouts  87.5 us (21%)
  matrix products  38 us (9%)
  between operations  13.9 us (3%)
  other arithmetic  12.5 us (3%)
    reduce_scatter x1, waiting for transfers between devices, on_device(): lax.psum_scatter(jnp.einsum('rnc,rnd->ncd', picked, slopes, preferred_ele...  126 us
    psum x1, waiting for transfers between devices, on_device(): weight_grad = lax.psum(summed, 'dp')  113 us
    all_gather x1, waiting for transfers between devices, on_device(): whole = lax.all_gather(weight_tiles, 'fsdp', axis=0, tiled=True)  25.9 us
    dot_general x1, matrix products, on_device(): jnp.einsum('rnc,rnd->ncd', picked, slopes, preferred_element_type=jnp.flo...  14.6 us
    gather x1, local copies, waits for them, and re-layouts, on_device(): taken = feature_blocks[:, columns_by_row]  13.2 us
    gather x1, local copies, waits for them, and re-layouts, on_device(): slopes_taken = slope_grad[:, rows_by_column]  12.5 us
    dot_general x1, matrix products, on_device(): jnp.einsum('rnkd,nkcd->rnc', slopes_taken, tiles_by_column, preferred_ele...  12.4 us
    gather x1, local copies, waits for them, and re-layouts, on_device(): tiles_by_row = whole[order_rows].reshape(nblocks, per_block, side, side)  12.1 us
  transfers between devices with their start and end apart: 3, of which 3 were waited for; matrix products, arithmetic and copies ran while one was open for 20% of the time, Pallas kernels for 0%

commit v1 on v0

v1 whole, which is shorter than its diff:
```python
import functools
import math

import jax
import jax.numpy as jnp
from jax import lax
from jax.experimental import pallas as pl
from jax.experimental.pallas import tpu as pltpu
from jax.sharding import PartitionSpec as P

SIDE_BLOCKS = 4
ROOT = math.sqrt(2.0 / math.pi)


def gelu_slope(value):
    square = value * value
    hyper = jnp.tanh(ROOT * (value + 0.044715 * square * value))
    return 0.5 * (1.0 + hyper) + 0.5 * value * (1.0 - hyper * hyper) * ROOT * (
        1.0 + 3.0 * 0.044715 * square
    )


def pattern(tile_row, tile_column, nblocks):
    total = tile_row.shape[0]
    mask = jnp.max(jnp.bitwise_xor(tile_row, tile_column))
    ids = jnp.arange(nblocks, dtype=jnp.int32)
    keys = jnp.bitwise_and(ids, ~mask) * nblocks + jnp.bitwise_and(ids, mask)

    def place(block):
        key = jnp.bitwise_and(block, ~mask) * nblocks + jnp.bitwise_and(block, mask)
        return jnp.sum((keys[None, :] < key[:, None]).astype(jnp.int32), axis=1)

    places = place(ids)
    blocks = jnp.sum(jnp.where(places[None, :] == ids[:, None], ids[None, :], 0), axis=1)
    at_row, at_column = place(tile_row), place(tile_column)
    slots = at_column * SIDE_BLOCKS + at_row % SIDE_BLOCKS
    every = jnp.arange(total, dtype=jnp.int32)
    tiles = jnp.sum(jnp.where(slots[None, :] == every[:, None], every[None, :], 0), axis=1)
    return blocks, tiles


def layer_kernel(steps, blocks, tiles, places, *refs):
    n, m = SIDE_BLOCKS, SIDE_BLOCKS * SIDE_BLOCKS
    feature_refs, grad_refs, tile_refs = refs[:n], refs[n : 2 * n], refs[2 * n : 2 * n + m]
    out_ref, partial_ref, out_buf, partial_buf, sems = refs[2 * n + m :]
    side = tile_refs[0].shape[1]
    step = pl.program_id(0)
    slot = lax.rem(step, 2)

    def copies(at, to):
        found = []
        for k in range(n):
            column = pl.multiple_of(blocks[at * n + k] * side, side)
            found.append(
                pltpu.make_async_copy(
                    out_buf.at[to, k], out_ref.at[:, pl.ds(column, side)], sems.at[to, k]
                )
            )
        for k in range(m):
            found.append(
                pltpu.make_async_copy(
                    partial_buf.at[to, k], partial_ref.at[places[at * m + k]], sems.at[to, n + k]
                )
            )
        return found

    @pl.when(step >= 2)
    def _():
        for copy in copies(step - 2, slot):
            copy.wait()

    feature = jnp.concatenate([ref[...] for ref in feature_refs], axis=1)
    grad = jnp.concatenate([ref[...] for ref in grad_refs], axis=1).astype(jnp.float32)
    weight = jnp.concatenate(
        [
            jnp.concatenate([tile_refs[c * n + r][0] for r in range(n)], axis=1)
            for c in range(n)
        ],
        axis=0,
    )
    preact = jnp.dot(feature, weight, preferred_element_type=jnp.float32)
    slope = (grad * gelu_slope(preact)).astype(jnp.bfloat16)
    back = lax.dot_general(
        slope, weight, (((1,), (1,)), ((), ())), preferred_element_type=jnp.float32
    )
    result = (grad + back).astype(jnp.bfloat16)
    term = lax.dot_general(
        feature, slope, (((0,), (0,)), ((), ())), preferred_element_type=jnp.float32
    ).astype(jnp.bfloat16)
    for k in range(n):
        out_buf[slot, k] = result[:, k * side : (k + 1) * side]
    for c in range(n):
        for r in range(n):
            partial_buf[slot, c * n + r] = term[
                c * side : (c + 1) * side, r * side : (r + 1) * side
            ]
    for copy in copies(step, slot):
        copy.start()

    @pl.when(step == steps - 1)
    def _():
        if steps > 1:
            for copy in copies(step - 1, 1 - slot):
                copy.wait()
        for copy in copies(step, slot):
            copy.wait()


def layer(features, grad_out, whole, blocks, tiles, places):
    rows, width = features.shape
    total, side, _ = whole.shape
    n, m = SIDE_BLOCKS, SIDE_BLOCKS * SIDE_BLOCKS
    steps = width // side // n

    def column(k):
        return pl.BlockSpec((rows, side), lambda g, b, t, p: (0, b[g * n + k]))

    def tile(k):
        return pl.BlockSpec((1, side, side), lambda g, b, t, p: (t[g * m + k], 0, 0))

    return pl.pallas_call(
        functools.partial(layer_kernel, steps),
        grid_spec=pltpu.PrefetchScalarGridSpec(
            num_scalar_prefetch=3,
            grid=(steps,),
            in_specs=[column(k) for k in range(n)] * 2 + [tile(k) for k in range(m)],
            out_specs=[pl.BlockSpec(memory_space=pl.ANY)] * 2,
            scratch_shapes=[
                pltpu.VMEM((2, n, rows, side), jnp.bfloat16),
                pltpu.VMEM((2, m, side, side), jnp.bfloat16),
                pltpu.SemaphoreType.DMA((2, n + m)),
            ],
        ),
        out_shape=[
            jax.ShapeDtypeStruct((rows, width), jnp.bfloat16),
            jax.ShapeDtypeStruct((total, side, side), jnp.bfloat16),
        ],
        compiler_params=pltpu.CompilerParams(
            dimension_semantics=("arbitrary",), vmem_limit_bytes=32 * 2**20
        ),
        cost_estimate=pl.CostEstimate(
            flops=6 * rows * width * n * side,
            bytes_accessed=6 * rows * width + 4 * total * side * side,
            transcendentals=rows * width,
        ),
        name="layer",
    )(blocks, tiles, places, *[features] * n, *[grad_out] * n, *[whole] * m)


def on_device(features, grad_out, weight_tiles, tile_row, tile_column):
    side = weight_tiles.shape[1]
    nblocks = features.shape[1] // side
    blocks, tiles = pattern(tile_row, tile_column, nblocks)
    whole = lax.all_gather(weight_tiles, "fsdp", axis=0, tiled=True)
    grad_features, partial = layer(features, grad_out, whole, blocks, tiles, tiles)
    summed = lax.psum_scatter(partial, "fsdp", scatter_dimension=0, tiled=True)
    weight_grad = lax.psum(summed.astype(jnp.float32), "dp")
    tile_update = weight_grad * lax.rsqrt(
        jnp.mean(weight_grad * weight_grad, axis=(1, 2), keepdims=True) + 1e-06
    )
    return (grad_features, tile_update)


def solution(mesh):
    return jax.shard_map(
        on_device,
        mesh=mesh,
        in_specs=(
            P(("dp", "fsdp"), None),
            P(("dp", "fsdp"), None),
            P("fsdp", None, None),
            P(),
            P(),
        ),
        out_specs=(P(("dp", "fsdp"), None), P("fsdp", None, None)),
        check_vma=False,
    )
```

time: 419 us -> 366 us (0.87)
  blocking collectives: 0 us -> 167 us
  waiting for transfers between devices: 266 us -> 131 us
  local copies, waits for them, and re-layouts: 87.5 us -> 7.52 us
  matrix products: 38 us -> 0 us
  Pallas kernels: 0 us -> 36.1 us
    psum x0 -> x1, blocking collectives: none -> 167 us  [on_device(): weight_grad = lax.psum(summed.astype(jnp.float32), 'dp')]
    psum x1 -> x0, waiting for transfers between devices: 113 us -> none  [on_device(): weight_grad = lax.psum(summed, 'dp')]
    gather x10 -> x0, local copies, waits for them, and re-layouts: 79.4 us -> none  [the longest x1 13.2 us: on_device(): taken = feature_blocks[:, columns_by_row]]
    reduce_scatter x1, waiting for transfers between devices: 126 us -> 72 us  [on_device(): summed = lax.psum_scatter(partial, 'fsdp', scatter_dimension=0, tiled=True)]
    dot_general x3 -> x0, matrix products: 38 us -> none  [the longest x1 14.6 us: on_device(): jnp.einsum('rnc,rnd->ncd', picked, slopes, preferred_element_type=jnp.flo...]
    pallas_call x0 -> x1, Pallas kernels: none -> 36.1 us  [layer(): pl.pallas_call(functools.partial(layer_kernel, steps), grid_spec=pltpu.Pr...]
    all_gather x1, waiting for transfers between devices: 25.9 us -> 58.1 us  [on_device(): whole = lax.all_gather(weight_tiles, 'fsdp', axis=0, tiled=True)]
    reshape x4 -> x0, local copies, waits for them, and re-layouts: 7.34 us -> none  [the longest x1 4.58 us: on_device(): grad_features = (grad_blocks.astype(jnp.float32) + returned).astype(jnp.b...]
  transfers between devices with their start and end apart: 3 -> 2, of which waited for: 3 -> 2; matrix products, arithmetic and copies ran while one was open for 20% -> 1% of each run, Pallas kernels for 0% -> 0%
where the time goes in v1:
time: 366 us
  blocking collectives  167 us (46%)
  waiting for transfers between devices  131 us (36%)
  Pallas kernels  36.1 us (10%)
  between operations  14.7 us (4%)
  other arithmetic  9.13 us (2%)
  local copies, waits for them, and re-layouts  7.52 us (2%)
    psum x1, blocking collectives, on_device(): weight_grad = lax.psum(summed.astype(jnp.float32), 'dp')  167 us
    reduce_scatter x1, waiting for transfers between devices, on_device(): summed = lax.psum_scatter(partial, 'fsdp', scatter_dimension=0, tiled=True)  72 us
    all_gather x1, waiting for transfers between devices, on_device(): whole = lax.all_gather(weight_tiles, 'fsdp', axis=0, tiled=True)  58.1 us
    pallas_call x1, Pallas kernels, layer(): pl.pallas_call(functools.partial(layer_kernel, steps), grid_spec=pltpu.Pr...  36.1 us
    unnamed x8, local copies, waits for them, and re-layouts  7.52 us
  transfers between devices with their start and end apart: 2, of which 2 were waited for; matrix products, arithmetic and copies ran while one was open for 1% of the time, Pallas kernels for 0%

profile of v1, /device:TPU:0, one launch (start us, length us, event | category | flops | bytes accessed | tf_op | source)
XLA Modules:
  0.0 365.7 jit_solution(13434514938853910429)
XLA Ops:
  7.2 0.0 all-gather.2.cloned.1.call-start
  7.2 0.7 all-gather.2.cloned.1.call-update
  7.9 0.0 reduce-scatter.2.cloned.1.call-start
  7.9 1.3 xor_reduce_fusion
  9.9 0.7 and_add_fusion.2
  10.6 0.2 convert_reduce_fusion.2
  10.8 0.1 select_reduce_fusion.1.blocks
  10.9 1.4 and_add_fusion
  12.2 0.1 convert_reduce_fusion.1
  12.3 0.1 select_reduce_fusion.tiles.places
  12.5 58.1 %all-gather.2.cloned.1.call-done.refs_8_.refs_9_.refs_10_.refs_11_.refs_12_.refs_13_.refs_14_.refs_15_.refs_16_.refs_17_.refs_18_.refs_19_.refs_20_.refs_21_.refs_22_.refs_23_ = bf16[256,128,128]{2,1,0:T(8,128)(2,1)} async-done(((bf16[64,128,128]{2,1,0:T(8,128)(2,1)}), bf16[256,128,128]{2,1,0:T(8,128)(2,1)}) %all-gather.2.cloned.1.call-update) | async-done | bytes 8388624 | tf_op jit(solution)/shard_map/all_gather | solution.py:154
  70.6 0.0 copy-start
  70.6 1.9 copy-done
  72.5 0.0 copy-start.1
  72.5 1.9 copy-done.1
  74.4 36.1 %layer.1 = (bf16[192,8192]{1,0:T(8,128)(2,1)}, bf16[256,128,128]{2,1,0:T(8,128)(2,1)S(1)}) custom-call(s32[64]{0:T(128)S(1)} %select_reduce_fusion.1.blocks, s32[256]{0:T(256)S(1)} %select_reduce_fusion.tiles.places, s32[256]{0:T(256)S(1)} %select_reduce_fusion.tiles.places, bf16[192,8192]{1,0:T(8,128)(2,1)S(1)} %copy-done, bf16[192,8192]{1,0:T(8,128)(2,1)S(1)} %copy-done, ...), custom_call_target="tpu_custom_call" | custom-call | flops 4831838208 | bytes 26214400 | tf_op jit(solution)/shard_map/layer/pallas_call | solution.py:121
  110.4 0.0 copy-start.2
  110.4 3.2 copy-done.2
  113.6 0.0 reduce-scatter.2.cloned.1.call-update
  113.7 72.0 %reduce-scatter.2.cloned.1.call-done = bf16[64,128,128]{2,1,0:T(8,128)(2,1)} async-done(((bf16[256,128,128]{2,1,0:T(8,128)(2,1)}), bf16[64,128,128]{2,1,0:T(8,128)(2,1)}) %reduce-scatter.2.cloned.1.call-update) | async-done | bytes 2097168 | tf_op jit(solution)/shard_map/reduce_scatter | solution.py:156
  185.7 167.4 %all-reduce.1 = f32[64,128,128]{2,1,0:T(8,128)} all-reduce(bf16[64,128,128]{2,1,0:T(8,128)(2,1)} %reduce-scatter.2.cloned.1.call-done), channel_id=1, replica_groups=mesh['dp'=8,'fsdp'=4] {'dp'}, use_global_device_ids=true, to_apply=%region_7.8 | all-reduce | flops 1048576 | bytes 6291456 | tf_op jit(solution)/shard_map/psum | solution.py:157
  353.0 0.0 copy-start.3
  353.0 2.9 multiply_reduce_fusion
  356.0 0.5 copy-done.3
  356.5 2.4 broadcast_multiply_fusion
  (2 shorter events, 0.0 us)
Async XLA Ops:
  7.2 63.4 %all-gather.2.cloned.1.call-start = ((), (), s32[]{:S(2)}) async-start(), calls=%async_computation.1 | async-start | bytes 10485760 | tf_op jit(solution)/shard_map/all_gather | solution.py:154
  7.9 177.8 %reduce-scatter.2.cloned.1.call-start = ((), (), s32[]{:S(2)}) async-start(), calls=%async_computation.2 | async-start | bytes 10485760 | tf_op jit(solution)/shard_map/reduce_scatter | solution.py:156
  70.6 1.9 copy-start
  72.5 1.9 copy-start.1
  110.4 3.2 copy-start.2
  353.0 3.4 copy-start.3
Sparse Core Ops, SparseCore 0:
  9.6 60.9 all-gather.1
  113.8 71.8 reduce-scatter.1

commit v2 on v1

--- a/solution.py
+++ b/solution.py
@@ -9,6 +9,7 @@
 from jax.sharding import PartitionSpec as P
 
 SIDE_BLOCKS = 4
+MESH = pl.DeviceIdType.MESH
 ROOT = math.sqrt(2.0 / math.pi)
 
 
@@ -147,23 +148,396 @@
     )(blocks, tiles, places, *[features] * n, *[grad_out] * n, *[whole] * m)
 
 
-def on_device(features, grad_out, weight_tiles, tile_row, tile_column):
-    side = weight_tiles.shape[1]
+class Place:
+    def __init__(self, n_dp, n_fsdp):
+        self.cores = 2
+        self.nx = n_fsdp // 2
+        self.ny = 2 if n_dp <= 8 else 4
+        self.nz = n_dp // self.ny
+
+    def locate(self):
+        fsdp, dp = lax.axis_index("fsdp"), lax.axis_index("dp")
+        self.x, self.c = fsdp // 2, fsdp % 2
+        self.z, self.y = dp // self.ny, dp % self.ny
+        return self
+
+    def at(self, x=None, c=None, y=None, z=None):
+        x = self.x if x is None else x
+        c = self.c if c is None else c
+        y = self.y if y is None else y
+        z = self.z if z is None else z
+        return (z * self.ny + y, x * 2 + c)
+
+    def step_x(self, k):
+        return lax.rem(self.x + k + self.nx, self.nx)
+
+    def step_y(self, k):
+        return lax.rem(self.y + k + self.ny, self.ny)
+
+    def step_z(self, k):
+        return lax.rem(self.z + k + self.nz, self.nz)
+
+    def x_peers(self):
+        return [self.at(x=self.step_x(k)) for k in range(1, self.nx)]
+
+    def y_peers(self):
+        return [self.at(y=self.step_y(k)) for k in range(1, self.ny)]
+
+    def z_peers(self):
+        return [self.at(z=self.step_z(k)) for k in range(1, self.nz)]
+
+
+def meet(peers):
+    barrier = pltpu.get_barrier_semaphore()
+    for peer in peers:
+        pl.semaphore_signal(barrier, inc=1, device_id=peer, device_id_type=MESH)
+    pl.semaphore_wait(barrier, len(peers))
+
+
+def remote(src, dst, send, recv, peer):
+    return pltpu.make_async_remote_copy(
+        src_ref=src, dst_ref=dst, send_sem=send, recv_sem=recv, device_id=peer, device_id_type=MESH
+    )
+
+
+def gather_kernel(
+    place, pieces, mine, whole, own_sem, xs, xr, ys, yr, cs, cr, ws, wr
+):
+    me = place.locate()
+    tiles = mine.shape[0]
+    part = tiles // me.ny
+    q = part // pieces
+    other = me.at(c=1 - me.c)
+    xp, yp = me.x_peers(), me.y_peers()
+    meet(xp + yp + [other])
+
+    def span(x, y, p):
+        return pl.ds((x * 2 + me.c) * tiles + y * part + p * q, q)
+
+    started = []
+
+    def go(copy):
+        copy.start()
+        started.append(copy)
+
+    for p in range(pieces):
+        for k in range(1, me.nx):
+            go(
+                remote(
+                    mine.at[pl.ds(me.y * part + p * q, q)],
+                    whole.at[span(me.x, me.y, p)],
+                    xs.at[k - 1, p],
+                    xr.at[k - 1, p],
+                    xp[k - 1],
+                )
+            )
+    home = pl.ds((me.x * 2 + me.c) * tiles, tiles)
+    go(remote(mine, whole.at[home], ws, wr, other))
+    local = pltpu.make_async_copy(mine, whole.at[home], own_sem)
+    local.start()
+
+    def to_other(x, y, k, j, p):
+        at = whole.at[span(x, y, p)]
+        go(remote(at, at, cs.at[k - 1, j, p], cr.at[k - 1, j, p], other))
+
+    for p in range(pieces):
+        for k in range(1, me.nx):
+            x = me.step_x(-k)
+            at = whole.at[span(x, me.y, p)]
+            remote(at, at, xs.at[k - 1, p], xr.at[k - 1, p], xp[k - 1]).wait_recv()
+            for j in range(1, me.ny):
+                go(remote(at, at, ys.at[k - 1, j - 1, p], yr.at[k - 1, j - 1, p], yp[j - 1]))
+            to_other(x, me.y, k, 0, p)
+    for p in range(pieces):
+        for k in range(1, me.nx):
+            x = me.step_x(-k)
+            for j in range(1, me.ny):
+                y = me.step_y(-j)
+                at = whole.at[span(x, y, p)]
+                remote(
+                    at, at, ys.at[k - 1, j - 1, p], yr.at[k - 1, j - 1, p], yp[j - 1]
+                ).wait_recv()
+                to_other(x, y, k, j, p)
+    local.wait()
+    away = whole.at[pl.ds((me.x * 2 + 1 - me.c) * tiles, tiles)]
+    remote(away, away, ws, wr, other).wait_recv()
+    for p in range(pieces):
+        for k in range(1, me.nx):
+            x = me.step_x(-k)
+            for j in range(me.ny):
+                y = me.step_y(-j)
+                at = whole.at[
+                    pl.ds((x * 2 + 1 - me.c) * tiles + y * part + p * q, q)
+                ]
+                remote(at, at, cs.at[k - 1, j, p], cr.at[k - 1, j, p], other).wait_recv()
+    for copy in started:
+        copy.wait_send()
+
+
+def gather_tiles(mine, place):
+    tiles, side, _ = mine.shape
+    part = tiles // place.ny
+    pieces = 4 if part % 4 == 0 else 1
+    nx, ny = place.nx, place.ny
+    dma = pltpu.SemaphoreType.DMA
+    return pl.pallas_call(
+        functools.partial(gather_kernel, place, pieces),
+        in_specs=[pl.BlockSpec(memory_space=pl.ANY)],
+        out_specs=pl.BlockSpec(memory_space=pl.ANY),
+        out_shape=jax.ShapeDtypeStruct((tiles * nx * 2, side, side), mine.dtype),
+        scratch_shapes=[
+            dma,
+            dma((nx - 1, pieces)),
+            dma((nx - 1, pieces)),
+            dma((nx - 1, ny - 1, pieces)),
+            dma((nx - 1, ny - 1, pieces)),
+            dma((nx - 1, ny, pieces)),
+            dma((nx - 1, ny, pieces)),
+            dma,
+            dma,
+        ],
+        compiler_params=pltpu.CompilerParams(collective_id=1, has_side_effects=True),
+        name="gather_tiles",
+    )(mine)
+
+
+def reduce_kernel(
+    place,
+    pieces,
+    q,
+    terms,
+    out,
+    own,
+    rc,
+    sx,
+    rx,
+    sy,
+    ry,
+    sz,
+    rz,
+    done,
+    own_sem,
+    cs,
+    cr,
+    xs,
+    xr,
+    ys,
+    yr,
+    zs,
+    zr,
+    keep_sem,
+    azs,
+    azr,
+    ays,
+    ayr,
+):
+    me = place.locate()
+    nx, ny, nz = me.nx, me.ny, me.nz
+    other = me.at(c=1 - me.c)
+    xp, yp, zp = me.x_peers(), me.y_peers(), me.z_peers()
+    meet([other] + xp + yp + zp)
+    started = []
+
+    def go(copy):
+        copy.start()
+        started.append(copy)
+
+    def wide(ref):
+        return ref[...].astype(jnp.float32)
+
+    def core_copy(p):
+        return remote(terms.at[1 - me.c, p], rc.at[p], cs.at[p], cr.at[p], other)
+
+    def own_copy(p):
+        return pltpu.make_async_copy(terms.at[me.c, p], own.at[p], own_sem.at[p])
+
+    def x_copy(p, k):
+        return remote(sx.at[p, k - 1], rx.at[p, k - 1], xs.at[p, k - 1], xr.at[p, k - 1], xp[k - 1])
+
+    def y_copy(p, j):
+        return remote(sy.at[p, j - 1], ry.at[p, j - 1], ys.at[p, j - 1], yr.at[p, j - 1], yp[j - 1])
+
+    def z_copy(p, m):
+        return remote(sz.at[p, m - 1], rz.at[p, m - 1], zs.at[p, m - 1], zr.at[p, m - 1], zp[m - 1])
+
+    def spread_z(p, m, z):
+        return remote(
+            done.at[p], out.at[p, me.y, z], azs.at[p, m - 1], azr.at[p, m - 1], zp[m - 1]
+        )
+
+    def spread_y(p, j, m, src, y, z):
+        return remote(
+            src, out.at[p, y, z], ays.at[p, j - 1, m], ayr.at[p, j - 1, m], yp[j - 1]
+        )
+
+    def keep_copy(p):
+        return pltpu.make_async_copy(done.at[p], out.at[p, me.y, me.z], keep_sem.at[p])
+
+    def over_x(p):
+        own_copy(p).wait()
+        core_copy(p).wait_recv()
+        for k in range(1, nx):
+            x = me.step_x(k)
+
+            def body(n, carry):
+                total = wide(own.at[p, x, n]) + wide(rc.at[p, x, n])
+                sx[p, k - 1, n] = total.astype(jnp.bfloat16)
+                return carry
+
+            lax.fori_loop(0, ny * nz * q, body, 0)
+            go(x_copy(p, k))
+
+    def up_to_x(p, n):
+        total = wide(own.at[p, me.x, n]) + wide(rc.at[p, me.x, n])
+        for k in range(1, nx):
+            total = total + wide(rx.at[p, k - 1, n])
+        return total
+
+    def up_to_y(p, n):
+        total = up_to_x(p, me.y * (nz * q) + n)
+        for j in range(1, ny):
+            total = total + wide(ry.at[p, j - 1, n])
+        return total
+
+    def over_y(p):
+        for k in range(1, nx):
+            x_copy(p, k).wait_recv()
+        for j in range(1, ny):
+            first = me.step_y(j) * (nz * q)
+
+            def body(n, carry):
+                sy[p, j - 1, n] = up_to_x(p, first + n).astype(jnp.bfloat16)
+                return carry
+
+            lax.fori_loop(0, nz * q, body, 0)
+            go(y_copy(p, j))
+
+    def over_z(p):
+        for j in range(1, ny):
+            y_copy(p, j).wait_recv()
+        for m in range(1, nz):
+            first = me.step_z(m) * q
+
+            def body(i, carry):
+                sz[p, m - 1, i] = up_to_y(p, first + i).astype(jnp.bfloat16)
+                return carry
+
+            lax.fori_loop(0, q, body, 0)
+            go(z_copy(p, m))
+
+    def finish(p):
+        for m in range(1, nz):
+            z_copy(p, m).wait_recv()
+
+        def body(i, carry):
+            total = up_to_y(p, me.z * q + i)
+            for m in range(1, nz):
+                total = total + wide(rz.at[p, m - 1, i])
+            scale = lax.rsqrt(jnp.mean(total * total, keepdims=True) + 1e-06)
+            done[p, i] = (total * scale).astype(jnp.bfloat16)
+            return carry
+
+        lax.fori_loop(0, q, body, 0)
+        for m in range(1, nz):
+            go(spread_z(p, m, me.z))
+        for j in range(1, ny):
+            go(spread_y(p, j, 0, done.at[p], me.y, me.z))
+        keep_copy(p).start()
+
+    def pass_on(p):
+        for m in range(1, nz):
+            z = me.step_z(-m)
+            spread_z(p, m, z).wait_recv()
+            for j in range(1, ny):
+                go(spread_y(p, j, m, out.at[p, me.y, z], me.y, z))
+
+    def collect(p):
+        for j in range(1, ny):
+            y = me.step_y(-j)
+            for m in range(nz):
+                z = me.step_z(-m)
+                spread_y(p, j, m, done.at[p], y, z).wait_recv()
+
+    for p in range(pieces):
+        go(core_copy(p))
+        own_copy(p).start()
+    stages = [over_x, over_y, over_z, finish, pass_on, collect]
+    for t in range(pieces + len(stages) - 1):
+        for s, stage in enumerate(stages):
+            if 0 <= t - s < pieces:
+                stage(t - s)
+    for p in range(pieces):
+        keep_copy(p).wait()
+    for copy in started:
+        copy.wait_send()
+
+
+def reduce_terms(terms, place, pieces, q):
+    side = terms.shape[-1]
+    nx, ny, nz = place.nx, place.ny, place.nz
+    n = ny * nz * q
+    dma = pltpu.SemaphoreType.DMA
+
+    def room(*lead):
+        return pltpu.VMEM((pieces,) + lead + (side, side), jnp.bfloat16)
+
+    return pl.pallas_call(
+        functools.partial(reduce_kernel, place, pieces, q),
+        in_specs=[pl.BlockSpec(memory_space=pl.ANY)],
+        out_specs=pl.BlockSpec(memory_space=pl.ANY),
+        out_shape=jax.ShapeDtypeStruct((pieces, ny, nz, q, side, side), jnp.bfloat16),
+        scratch_shapes=[
+            room(nx, n),
+            room(nx, n),
+            room(nx - 1, n),
+            room(nx - 1, n),
+            room(ny - 1, nz * q),
+            room(ny - 1, nz * q),
+            room(nz - 1, q),
+            room(nz - 1, q),
+            room(q),
+            dma((pieces,)),
+            dma((pieces,)),
+            dma((pieces,)),
+            dma((pieces, nx - 1)),
+            dma((pieces, nx - 1)),
+            dma((pieces, ny - 1)),
+            dma((pieces, ny - 1)),
+            dma((pieces, nz - 1)),
+            dma((pieces, nz - 1)),
+            dma((pieces,)),
+            dma((pieces, nz - 1)),
+            dma((pieces, nz - 1)),
+            dma((pieces, ny - 1, nz)),
+            dma((pieces, ny - 1, nz)),
+        ],
+        compiler_params=pltpu.CompilerParams(
+            collective_id=2, has_side_effects=True, vmem_limit_bytes=40 * 2**20
+        ),
+        name="reduce_terms",
+    )(terms)
+
+
+def on_device(n_dp, n_fsdp, features, grad_out, weight_tiles, tile_row, tile_column):
+    tiles_here, side, _ = weight_tiles.shape
     nblocks = features.shape[1] // side
+    place = Place(n_dp, n_fsdp)
+    nx, n = place.nx, place.ny * place.nz
+    pieces = max(count for count in (1, 2, 4, 8) if tiles_here % (n * count) == 0)
+    n = tiles_here // pieces
     blocks, tiles = pattern(tile_row, tile_column, nblocks)
-    whole = lax.all_gather(weight_tiles, "fsdp", axis=0, tiled=True)
-    grad_features, partial = layer(features, grad_out, whole, blocks, tiles, tiles)
-    summed = lax.psum_scatter(partial, "fsdp", scatter_dimension=0, tiled=True)
-    weight_grad = lax.psum(summed.astype(jnp.float32), "dp")
-    tile_update = weight_grad * lax.rsqrt(
-        jnp.mean(weight_grad * weight_grad, axis=(1, 2), keepdims=True) + 1e-06
-    )
-    return (grad_features, tile_update)
+    owner, rest = tiles // tiles_here, tiles % tiles_here
+    places = ((owner % 2 * pieces + rest // n) * nx + owner // 2) * n + rest % n
+    whole = gather_tiles(weight_tiles, place)
+    grad_features, partial = layer(features, grad_out, whole, blocks, tiles, places)
+    terms = partial.reshape(2, pieces, nx, n, side, side)
+    tile_update = reduce_terms(terms, place, pieces, n // (place.ny * place.nz))
+    return (grad_features, tile_update.reshape(tiles_here, side, side).astype(jnp.float32))
 
 
 def solution(mesh):
     return jax.shard_map(
-        on_device,
+        functools.partial(on_device, mesh.shape["dp"], mesh.shape["fsdp"]),
         mesh=mesh,
         in_specs=(
             P(("dp", "fsdp"), None),

time: 366 us -> 189 us (0.52)
  blocking collectives: 167 us -> 0 us
  Pallas kernels: 36.1 us -> 178 us
  waiting for transfers between devices: 131 us -> 0 us
  between operations: 14.7 us -> 1.35 us
  local copies, waits for them, and re-layouts: 7.52 us -> 1.89 us
    psum x1 -> x0, blocking collectives: 167 us -> none  [on_device(): weight_grad = lax.psum(summed.astype(jnp.float32), 'dp')]
    pallas_call x0 -> x2, Pallas kernels: none -> 142 us  [the longest x1 74.4 us: reduce_terms(): pl.pallas_call(functools.partial(reduce_kernel, place, pieces, q), in_spe...]
    reduce_scatter x1 -> x0, waiting for transfers between devices: 72 us -> none  [on_device(): summed = lax.psum_scatter(partial, 'fsdp', scatter_dimension=0, tiled=True)]
    all_gather x1 -> x0, waiting for transfers between devices: 58.1 us -> none  [on_device(): whole = lax.all_gather(weight_tiles, 'fsdp', axis=0, tiled=True)]
    unnamed x8 -> x4, local copies, waits for them, and re-layouts: 7.52 us -> 1.89 us
  transfers between devices with their start and end apart: 2 -> 0, of which waited for: 2 -> 0; matrix products, arithmetic and copies ran while one was open for 1% -> 0% of each run, Pallas kernels for 0% -> 0%
where the time goes in v2:
time: 189 us; the launch traced here: 188 us
  Pallas kernels  178 us (94%)
  other arithmetic  6.55 us (3%)
    pallas_call x1, Pallas kernels, reduce_terms(): pl.pallas_call(functools.partial(reduce_kernel, place, pieces, q), in_spe...  74.4 us
    pallas_call x1, Pallas kernels, gather_tiles(): pl.pallas_call(functools.partial(gather_kernel, place, pieces), in_specs=...  68 us
    pallas_call x1, Pallas kernels, layer(): pl.pallas_call(functools.partial(layer_kernel, steps), grid_spec=pltpu.Pr...  36.1 us

profile of v2, /device:TPU:0, one launch (start us, length us, event | category | flops | bytes accessed | tf_op | source)
XLA Modules:
  0.0 188.2 jit_solution(16793592022799635)
XLA Ops:
  0.6 1.3 xor_reduce_fusion
  2.6 0.7 and_add_fusion.2
  3.3 0.2 convert_reduce_fusion.2
  3.4 0.1 select_reduce_fusion.1.blocks
  3.6 1.4 and_add_fusion
  4.9 0.1 convert_reduce_fusion.1
  5.0 0.1 select_reduce_fusion.tiles
  5.2 0.0 copy-start
  5.2 68.0 %gather_tiles.1.refs_8_.refs_9_.refs_10_.refs_11_.refs_12_.refs_13_.refs_14_.refs_15_.refs_16_.refs_17_.refs_18_.refs_19_.refs_20_.refs_21_.refs_22_.refs_23_ = bf16[256,128,128]{2,1,0:T(8,128)(2,1)} custom-call(bf16[64,128,128]{2,1,0:T(8,128)(2,1)} %mine.1), custom_call_target="tpu_custom_call" | custom-call | tf_op jit(solution)/shard_map/gather_tiles/pallas_call | solution.py:283
  73.2 0.0 copy-done
  73.2 0.0 copy-start.1
  73.2 1.9 copy-done.1
  75.1 36.1 %layer.1 = (bf16[192,8192]{1,0:T(8,128)(2,1)}, bf16[256,128,128]{2,1,0:T(8,128)(2,1)S(1)}) custom-call(s32[64]{0:T(128)S(1)} %select_reduce_fusion.1.blocks, s32[256]{0:T(256)S(1)} %select_reduce_fusion.tiles, s32[256]{0:T(256)S(1)} %fusion.4.places, bf16[192,8192]{1,0:T(8,128)(2,1)S(1)} %copy-done, bf16[192,8192]{1,0:T(8,128)(2,1)S(1)} %copy-done, ...), custom_call_target="tpu_custom_call" | custom-call | flops 4831838208 | bytes 26214400 | tf_op jit(solution)/shard_map/layer/pallas_call | solution.py:122
  111.2 74.4 %reduce_terms.1 = bf16[8,2,4,1,128,128]{5,4,3,2,1,0:T(8,128)(2,1)S(1)} custom-call(bf16[2,8,2,8,128,128]{5,4,3,2,1,0:T(8,128)(2,1)S(1)} %bitcast.4), custom_call_target="tpu_custom_call" | custom-call | tf_op jit(solution)/shard_map/reduce_terms/pallas_call | solution.py:484
  185.5 2.7 %bitcast_convert_fusion = f32[64,128,128]{2,1,0:T(8,128)} fusion(bf16[8,2,4,1,128,128]{5,4,3,2,1,0:T(8,128)(2,1)S(1)} %reduce_terms.1), kind=kLoop, calls=%fused_computation | loop fusion | flops 1048576 | bytes 6291456 | tf_op jit(solution)/shard_map/convert_element_type | solution.py:535
  (2 shorter events, 0.0 us)
Async XLA Ops:
  5.2 68.0 %copy-start = (bf16[192,8192]{1,0:T(8,128)(2,1)S(1)}, bf16[192,8192]{1,0:T(8,128)(2,1)}, u32[]{:S(2)}) copy-start(bf16[192,8192]{1,0:T(8,128)(2,1)} %refs_3_.1) | copy-start | bytes 9437188
  73.2 1.9 %copy-start.1 = (bf16[192,8192]{1,0:T(8,128)(2,1)S(1)}, bf16[192,8192]{1,0:T(8,128)(2,1)}, u32[]{:S(2)}) copy-start(bf16[192,8192]{1,0:T(8,128)(2,1)} %refs_7_.1) | copy-start | bytes 9437188

commit v3 on v2

--- a/solution.py
+++ b/solution.py
@@ -10,6 +10,7 @@
 
 SIDE_BLOCKS = 4
 MESH = pl.DeviceIdType.MESH
+WINDOW = 3
 ROOT = math.sqrt(2.0 / math.pi)
 
 
@@ -40,71 +41,64 @@
     return blocks, tiles
 
 
-def layer_kernel(steps, blocks, tiles, places, *refs):
+def layer_kernel(steps, blocks, tiles, places, features, grads, whole, out_ref, partial_ref, term_buf, sems):
     n, m = SIDE_BLOCKS, SIDE_BLOCKS * SIDE_BLOCKS
-    feature_refs, grad_refs, tile_refs = refs[:n], refs[n : 2 * n], refs[2 * n : 2 * n + m]
-    out_ref, partial_ref, out_buf, partial_buf, sems = refs[2 * n + m :]
-    side = tile_refs[0].shape[1]
-    step = pl.program_id(0)
-    slot = lax.rem(step, 2)
-
-    def copies(at, to):
-        found = []
-        for k in range(n):
-            column = pl.multiple_of(blocks[at * n + k] * side, side)
-            found.append(
-                pltpu.make_async_copy(
-                    out_buf.at[to, k], out_ref.at[:, pl.ds(column, side)], sems.at[to, k]
-                )
-            )
+    side = whole.shape[1]
+
+    def drain(slot):
+        pltpu.make_async_copy(
+            term_buf.at[slot], partial_ref.at[pl.ds(0, m)], sems.at[slot]
+        ).wait()
+
+    def group(g, slot):
+        columns = [
+            pl.ds(pl.multiple_of(blocks[g * n + k] * side, side), side) for k in range(n)
+        ]
+        feature = jnp.concatenate([features[:, at] for at in columns], axis=1)
+        grad = jnp.concatenate([grads[:, at] for at in columns], axis=1).astype(jnp.float32)
+        weight = jnp.concatenate(
+            [
+                jnp.concatenate([whole[tiles[g * m + c * n + r]] for r in range(n)], axis=1)
+                for c in range(n)
+            ],
+            axis=0,
+        )
+        preact = jnp.dot(feature, weight, preferred_element_type=jnp.float32)
+        slope = (grad * gelu_slope(preact)).astype(jnp.bfloat16)
+        back = lax.dot_general(
+            slope, weight, (((1,), (1,)), ((), ())), preferred_element_type=jnp.float32
+        )
+        result = (grad + back).astype(jnp.bfloat16)
+        for k, at in enumerate(columns):
+            out_ref[:, at] = result[:, k * side : (k + 1) * side]
+        term = lax.dot_general(
+            feature, slope, (((0,), (0,)), ((), ())), preferred_element_type=jnp.float32
+        )
+        for c in range(n):
+            for r in range(n):
+                term_buf[slot, c * n + r] = term[
+                    c * side : (c + 1) * side, r * side : (r + 1) * side
+                ]
         for k in range(m):
-            found.append(
-                pltpu.make_async_copy(
-                    partial_buf.at[to, k], partial_ref.at[places[at * m + k]], sems.at[to, n + k]
-                )
-            )
-        return found
-
-    @pl.when(step >= 2)
-    def _():
-        for copy in copies(step - 2, slot):
-            copy.wait()
-
-    feature = jnp.concatenate([ref[...] for ref in feature_refs], axis=1)
-    grad = jnp.concatenate([ref[...] for ref in grad_refs], axis=1).astype(jnp.float32)
-    weight = jnp.concatenate(
-        [
-            jnp.concatenate([tile_refs[c * n + r][0] for r in range(n)], axis=1)
-            for c in range(n)
-        ],
-        axis=0,
-    )
-    preact = jnp.dot(feature, weight, preferred_element_type=jnp.float32)
-    slope = (grad * gelu_slope(preact)).astype(jnp.bfloat16)
-    back = lax.dot_general(
-        slope, weight, (((1,), (1,)), ((), ())), preferred_element_type=jnp.float32
-    )
-    result = (grad + back).astype(jnp.bfloat16)
-    term = lax.dot_general(
-        feature, slope, (((0,), (0,)), ((), ())), preferred_element_type=jnp.float32
-    ).astype(jnp.bfloat16)
-    for k in range(n):
-        out_buf[slot, k] = result[:, k * side : (k + 1) * side]
-    for c in range(n):
-        for r in range(n):
-            partial_buf[slot, c * n + r] = term[
-                c * side : (c + 1) * side, r * side : (r + 1) * side
-            ]
-    for copy in copies(step, slot):
-        copy.start()
-
-    @pl.when(step == steps - 1)
-    def _():
-        if steps > 1:
-            for copy in copies(step - 1, 1 - slot):
-                copy.wait()
-        for copy in copies(step, slot):
-            copy.wait()
+            pltpu.make_async_copy(
+                term_buf.at[slot, k], partial_ref.at[places[g * m + k]], sems.at[slot]
+            ).start()
+
+    slots = term_buf.shape[0]
+
+    def body(i, carry):
+        for k in range(slots):
+
+            @pl.when(i > 0)
+            def _():
+                drain(k)
+
+            group(i * slots + k, k)
+        return carry
+
+    lax.fori_loop(0, steps // slots, body, 0)
+    for k in range(slots):
+        drain(k)
 
 
 def layer(features, grad_out, whole, blocks, tiles, places):
@@ -112,40 +106,29 @@
     total, side, _ = whole.shape
     n, m = SIDE_BLOCKS, SIDE_BLOCKS * SIDE_BLOCKS
     steps = width // side // n
-
-    def column(k):
-        return pl.BlockSpec((rows, side), lambda g, b, t, p: (0, b[g * n + k]))
-
-    def tile(k):
-        return pl.BlockSpec((1, side, side), lambda g, b, t, p: (t[g * m + k], 0, 0))
-
+    slots = 2 if steps % 2 == 0 else 1
+    vmem = pl.BlockSpec(memory_space=pltpu.VMEM)
+    smem = pl.BlockSpec(memory_space=pltpu.SMEM)
     return pl.pallas_call(
         functools.partial(layer_kernel, steps),
-        grid_spec=pltpu.PrefetchScalarGridSpec(
-            num_scalar_prefetch=3,
-            grid=(steps,),
-            in_specs=[column(k) for k in range(n)] * 2 + [tile(k) for k in range(m)],
-            out_specs=[pl.BlockSpec(memory_space=pl.ANY)] * 2,
-            scratch_shapes=[
-                pltpu.VMEM((2, n, rows, side), jnp.bfloat16),
-                pltpu.VMEM((2, m, side, side), jnp.bfloat16),
-                pltpu.SemaphoreType.DMA((2, n + m)),
-            ],
-        ),
+        in_specs=[smem] * 3 + [vmem] * 3,
+        out_specs=[vmem, pl.BlockSpec(memory_space=pl.ANY)],
+        scratch_shapes=[
+            pltpu.VMEM((slots, m, side, side), jnp.float32),
+            pltpu.SemaphoreType.DMA((slots,)),
+        ],
         out_shape=[
             jax.ShapeDtypeStruct((rows, width), jnp.bfloat16),
-            jax.ShapeDtypeStruct((total, side, side), jnp.bfloat16),
+            jax.ShapeDtypeStruct((total, side, side), jnp.float32),
         ],
-        compiler_params=pltpu.CompilerParams(
-            dimension_semantics=("arbitrary",), vmem_limit_bytes=32 * 2**20
-        ),
+        compiler_params=pltpu.CompilerParams(vmem_limit_bytes=26 * 2**20),
         cost_estimate=pl.CostEstimate(
             flops=6 * rows * width * n * side,
-            bytes_accessed=6 * rows * width + 4 * total * side * side,
+            bytes_accessed=6 * rows * width + 6 * total * side * side,
             transcendentals=rows * width,
         ),
         name="layer",
-    )(blocks, tiles, places, *[features] * n, *[grad_out] * n, *[whole] * m)
+    )(blocks, tiles, places, features, grad_out, whole)
 
 
 class Place:
@@ -220,48 +203,69 @@
         copy.start()
         started.append(copy)
 
-    for p in range(pieces):
-        for k in range(1, me.nx):
-            go(
-                remote(
-                    mine.at[pl.ds(me.y * part + p * q, q)],
-                    whole.at[span(me.x, me.y, p)],
-                    xs.at[k - 1, p],
-                    xr.at[k - 1, p],
-                    xp[k - 1],
-                )
-            )
-    home = pl.ds((me.x * 2 + me.c) * tiles, tiles)
-    go(remote(mine, whole.at[home], ws, wr, other))
-    local = pltpu.make_async_copy(mine, whole.at[home], own_sem)
-    local.start()
+    def x_copy(p, k):
+        return remote(
+            mine.at[pl.ds(me.y * part + p * q, q)],
+            whole.at[span(me.x, me.y, p)],
+            xs.at[k - 1, p],
+            xr.at[k - 1, p],
+            xp[k - 1],
+        )
+
+    def home(core, p):
+        return pl.ds((me.x * 2 + core) * tiles + p * q * me.ny, q * me.ny)
+
+    def own_copy(p):
+        src = mine.at[pl.ds(p * q * me.ny, q * me.ny)]
+        return pltpu.make_async_copy(src, whole.at[home(me.c, p)], own_sem.at[p])
+
+    def core_copy(p):
+        src = mine.at[pl.ds(p * q * me.ny, q * me.ny)]
+        return remote(src, whole.at[home(me.c, p)], ws.at[p], wr.at[p], other)
 
     def to_other(x, y, k, j, p):
         at = whole.at[span(x, y, p)]
         go(remote(at, at, cs.at[k - 1, j, p], cr.at[k - 1, j, p], other))
 
-    for p in range(pieces):
+    def y_copy(p, k, j, y):
+        at = whole.at[span(me.step_x(-k), y, p)]
+        return remote(at, at, ys.at[k - 1, j - 1, p], yr.at[k - 1, j - 1, p], yp[j - 1])
+
+    def land_x(p):
         for k in range(1, me.nx):
             x = me.step_x(-k)
-            at = whole.at[span(x, me.y, p)]
-            remote(at, at, xs.at[k - 1, p], xr.at[k - 1, p], xp[k - 1]).wait_recv()
+            x_copy(p, k).wait_send()
+            remote(
+                mine.at[pl.ds(0, q)], whole.at[span(x, me.y, p)], xs.at[k - 1, p], xr.at[k - 1, p], xp[k - 1]
+            ).wait_recv()
+            if p + WINDOW < pieces:
+                x_copy(p + WINDOW, k).start()
             for j in range(1, me.ny):
-                go(remote(at, at, ys.at[k - 1, j - 1, p], yr.at[k - 1, j - 1, p], yp[j - 1]))
+                go(y_copy(p, k, j, me.y))
             to_other(x, me.y, k, 0, p)
-    for p in range(pieces):
+        go(core_copy(p))
+        own_copy(p).start()
+
+    def land_y(p):
         for k in range(1, me.nx):
             x = me.step_x(-k)
             for j in range(1, me.ny):
                 y = me.step_y(-j)
-                at = whole.at[span(x, y, p)]
-                remote(
-                    at, at, ys.at[k - 1, j - 1, p], yr.at[k - 1, j - 1, p], yp[j - 1]
-                ).wait_recv()
+                y_copy(p, k, j, y).wait_recv()
                 to_other(x, y, k, j, p)
-    local.wait()
-    away = whole.at[pl.ds((me.x * 2 + 1 - me.c) * tiles, tiles)]
-    remote(away, away, ws, wr, other).wait_recv()
+
+    for p in range(min(WINDOW, pieces)):
+        for k in range(1, me.nx):
+            x_copy(p, k).start()
+    for t in range(pieces + 1):
+        if t < pieces:
+            land_x(t)
+        if t >= 1:
+            land_y(t - 1)
     for p in range(pieces):
+        own_copy(p).wait()
+        away = whole.at[home(1 - me.c, p)]
+        remote(away, away, ws.at[p], wr.at[p], other).wait_recv()
         for k in range(1, me.nx):
             x = me.step_x(-k)
             for j in range(me.ny):
@@ -277,7 +281,7 @@
 def gather_tiles(mine, place):
     tiles, side, _ = mine.shape
     part = tiles // place.ny
-    pieces = 4 if part % 4 == 0 else 1
+    pieces = 8 if part % 8 == 0 else 1
     nx, ny = place.nx, place.ny
     dma = pltpu.SemaphoreType.DMA
     return pl.pallas_call(
@@ -286,15 +290,15 @@
         out_specs=pl.BlockSpec(memory_space=pl.ANY),
         out_shape=jax.ShapeDtypeStruct((tiles * nx * 2, side, side), mine.dtype),
         scratch_shapes=[
-            dma,
+            dma((pieces,)),
             dma((nx - 1, pieces)),
             dma((nx - 1, pieces)),
             dma((nx - 1, ny - 1, pieces)),
             dma((nx - 1, ny - 1, pieces)),
             dma((nx - 1, ny, pieces)),
             dma((nx - 1, ny, pieces)),
-            dma,
-            dma,
+            dma((pieces,)),
+            dma((pieces,)),
         ],
         compiler_params=pltpu.CompilerParams(collective_id=1, has_side_effects=True),
         name="gather_tiles",
@@ -376,6 +380,10 @@
     def over_x(p):
         own_copy(p).wait()
         core_copy(p).wait_recv()
+        if p + WINDOW < pieces:
+            core_copy(p).wait_send()
+            core_copy(p + WINDOW).start()
+            own_copy(p + WINDOW).start()
         for k in range(1, nx):
             x = me.step_x(k)
 
@@ -458,8 +466,8 @@
                 z = me.step_z(-m)
                 spread_y(p, j, m, done.at[p], y, z).wait_recv()
 
-    for p in range(pieces):
-        go(core_copy(p))
+    for p in range(min(WINDOW, pieces)):
+        core_copy(p).start()
         own_copy(p).start()
     stages = [over_x, over_y, over_z, finish, pass_on, collect]
     for t in range(pieces + len(stages) - 1):
@@ -468,6 +476,8 @@
                 stage(t - s)
     for p in range(pieces):
         keep_copy(p).wait()
+        if p + WINDOW >= pieces:
+            core_copy(p).wait_send()
     for copy in started:
         copy.wait_send()
 
@@ -478,8 +488,8 @@
     n = ny * nz * q
     dma = pltpu.SemaphoreType.DMA
 
-    def room(*lead):
-        return pltpu.VMEM((pieces,) + lead + (side, side), jnp.bfloat16)
+    def room(*lead, dtype=jnp.bfloat16):
+        return pltpu.VMEM((pieces,) + lead + (side, side), dtype)
 
     return pl.pallas_call(
         functools.partial(reduce_kernel, place, pieces, q),
@@ -487,8 +497,8 @@
         out_specs=pl.BlockSpec(memory_space=pl.ANY),
         out_shape=jax.ShapeDtypeStruct((pieces, ny, nz, q, side, side), jnp.bfloat16),
         scratch_shapes=[
-            room(nx, n),
-            room(nx, n),
+            room(nx, n, dtype=jnp.float32),
+            room(nx, n, dtype=jnp.float32),
             room(nx - 1, n),
             room(nx - 1, n),
             room(ny - 1, nz * q),
@@ -512,7 +522,7 @@
             dma((pieces, ny - 1, nz)),
         ],
         compiler_params=pltpu.CompilerParams(
-            collective_id=2, has_side_effects=True, vmem_limit_bytes=40 * 2**20
+            collective_id=2, has_side_effects=True, vmem_limit_bytes=48 * 2**20
         ),
         name="reduce_terms",
     )(terms)

time: 189 us -> 181 us (0.958)
  Pallas kernels: 178 us -> 167 us
  local copies, waits for them, and re-layouts: 1.89 us -> 5.27 us
    pallas_call x1, Pallas kernels: 36.1 us -> 17.4 us  [layer(): pl.pallas_call(functools.partial(layer_kernel, steps), in_specs=[smem] *...]
    pallas_call x1, Pallas kernels: 68 us -> 74.6 us  [gather_tiles(): pl.pallas_call(functools.partial(gather_kernel, place, pieces), in_specs=...]
    unnamed x4 -> x6, local copies, waits for them, and re-layouts: 1.89 us -> 5.27 us
where the time goes in v3:
time: 181 us
  Pallas kernels  167 us (92%)
  other arithmetic  6.55 us (4%)
  local copies, waits for them, and re-layouts  5.27 us (3%)
    pallas_call x1, Pallas kernels, reduce_terms(): pl.pallas_call(functools.partial(reduce_kernel, place, pieces, q), in_spe...  75.4 us
    pallas_call x1, Pallas kernels, gather_tiles(): pl.pallas_call(functools.partial(gather_kernel, place, pieces), in_specs=...  74.6 us
    pallas_call x1, Pallas kernels, layer(): pl.pallas_call(functools.partial(layer_kernel, steps), in_specs=[smem] *...  17.4 us
    unnamed x6, local copies, waits for them, and re-layouts  5.27 us

profile of v3, /device:TPU:0, one launch (start us, length us, event | category | flops | bytes accessed | tf_op | source)
XLA Modules:
  0.0 180.6 jit_solution(12394749947154270415)
XLA Ops:
  0.6 1.3 xor_reduce_fusion
  2.6 0.7 and_add_fusion.2
  3.3 0.2 convert_reduce_fusion.2
  3.4 0.1 select_reduce_fusion.1.blocks
  3.6 1.4 and_add_fusion
  4.9 0.1 convert_reduce_fusion.1
  5.0 0.1 select_reduce_fusion.tiles
  5.2 0.0 copy-start.1
  5.2 74.6 %gather_tiles.1.whole = bf16[256,128,128]{2,1,0:T(8,128)(2,1)} custom-call(bf16[64,128,128]{2,1,0:T(8,128)(2,1)} %mine.1), custom_call_target="tpu_custom_call" | custom-call | tf_op jit(solution)/shard_map/gather_tiles/pallas_call | solution.py:287
  79.8 0.0 copy-done.1
  79.8 0.0 copy-start
  79.9 3.4 %copy-done = bf16[256,128,128]{2,1,0:T(8,128)(2,1)S(1)} copy-done((bf16[256,128,128]{2,1,0:T(8,128)(2,1)S(1)}, bf16[256,128,128]{2,1,0:T(8,128)(2,1)}, u32[]{:S(2)}) %copy-start) | copy-done | bytes 8388632
  83.2 0.0 copy-start.2
  83.2 1.9 %copy-done.2 = bf16[192,8192]{1,0:T(8,128)(2,1)S(1)} copy-done((bf16[192,8192]{1,0:T(8,128)(2,1)S(1)}, bf16[192,8192]{1,0:T(8,128)(2,1)}, u32[]{:S(2)}) %copy-start.2) | copy-done | bytes 3145752
  85.1 17.4 %layer.1 = (bf16[192,8192]{1,0:T(8,128)(2,1)}, f32[256,128,128]{2,1,0:T(8,128)}) custom-call(s32[64]{0:T(128)S(1)} %select_reduce_fusion.1.blocks, s32[256]{0:T(256)S(1)} %select_reduce_fusion.tiles, s32[256]{0:T(256)S(1)} %fusion.4.places, bf16[192,8192]{1,0:T(8,128)(2,1)S(1)} %copy-done.1, bf16[192,8192]{1,0:T(8,128)(2,1)S(1)} %copy-done.2, ...), custom_call_target="tpu_custom_call" | custom-call | flops 4831838208 | bytes 34603008 | tf_op jit(solution)/shard_map/layer/pallas_call | solution.py:112
  102.5 75.4 %reduce_terms.1 = bf16[8,2,4,1,128,128]{5,4,3,2,1,0:T(8,128)(2,1)S(1)} custom-call(f32[2,8,2,8,128,128]{5,4,3,2,1,0:T(8,128)} %bitcast.4), custom_call_target="tpu_custom_call" | custom-call | tf_op jit(solution)/shard_map/reduce_terms/pallas_call | solution.py:494
  177.9 2.7 %bitcast_convert_fusion = f32[64,128,128]{2,1,0:T(8,128)} fusion(bf16[8,2,4,1,128,128]{5,4,3,2,1,0:T(8,128)(2,1)S(1)} %reduce_terms.1), kind=kLoop, calls=%fused_computation | loop fusion | flops 1048576 | bytes 6291456 | tf_op jit(solution)/shard_map/convert_element_type | solution.py:545
  (2 shorter events, 0.0 us)
Async XLA Ops:
  5.2 74.7 %copy-start.1 = (bf16[192,8192]{1,0:T(8,128)(2,1)S(1)}, bf16[192,8192]{1,0:T(8,128)(2,1)}, u32[]{:S(2)}) copy-start(bf16[192,8192]{1,0:T(8,128)(2,1)} %features.1) | copy-start | bytes 9437188
  79.8 3.4 %copy-start = (bf16[256,128,128]{2,1,0:T(8,128)(2,1)S(1)}, bf16[256,128,128]{2,1,0:T(8,128)(2,1)}, u32[]{:S(2)}) copy-start(bf16[256,128,128]{2,1,0:T(8,128)(2,1)} %gather_tiles.1.whole) | copy-start | bytes 25165828
  83.2 1.9 %copy-start.2 = (bf16[192,8192]{1,0:T(8,128)(2,1)S(1)}, bf16[192,8192]{1,0:T(8,128)(2,1)}, u32[]{:S(2)}) copy-start(bf16[192,8192]{1,0:T(8,128)(2,1)} %grads.1) | copy-start | bytes 9437188

commit v4 on v3

--- a/solution.py
+++ b/solution.py
@@ -286,8 +286,8 @@
     dma = pltpu.SemaphoreType.DMA
     return pl.pallas_call(
         functools.partial(gather_kernel, place, pieces),
-        in_specs=[pl.BlockSpec(memory_space=pl.ANY)],
-        out_specs=pl.BlockSpec(memory_space=pl.ANY),
+        in_specs=[pl.BlockSpec(memory_space=pltpu.VMEM)],
+        out_specs=pl.BlockSpec(memory_space=pltpu.VMEM),
         out_shape=jax.ShapeDtypeStruct((tiles * nx * 2, side, side), mine.dtype),
         scratch_shapes=[
             dma((pieces,)),
@@ -300,7 +300,9 @@
             dma((pieces,)),
             dma((pieces,)),
         ],
-        compiler_params=pltpu.CompilerParams(collective_id=1, has_side_effects=True),
+        compiler_params=pltpu.CompilerParams(
+            collective_id=1, has_side_effects=True, vmem_limit_bytes=24 * 2**20
+        ),
         name="gather_tiles",
     )(mine)
 

time: 181 us -> 137 us (0.76)
  Pallas kernels: 167 us -> 127 us
  local copies, waits for them, and re-layouts: 5.27 us -> 1.59 us
    pallas_call x1, Pallas kernels: 74.6 us -> 33.9 us  [gather_tiles(): pl.pallas_call(functools.partial(gather_kernel, place, pieces), in_specs=...]
    unnamed x6, local copies, waits for them, and re-layouts: 5.27 us -> 1.59 us
where the time goes in v4:
time: 137 us
  Pallas kernels  127 us (93%)
  other arithmetic  6.55 us (5%)
  local copies, waits for them, and re-layouts  1.59 us (1%)
    pallas_call x1, Pallas kernels, reduce_terms(): pl.pallas_call(functools.partial(reduce_kernel, place, pieces, q), in_spe...  76.1 us
    pallas_call x1, Pallas kernels, gather_tiles(): pl.pallas_call(functools.partial(gather_kernel, place, pieces), in_specs=...  33.9 us
    pallas_call x1, Pallas kernels, layer(): pl.pallas_call(functools.partial(layer_kernel, steps), in_specs=[smem] *...  17.5 us

profile of v4, /device:TPU:0, one launch (start us, length us, event | category | flops | bytes accessed | tf_op | source)
XLA Modules:
  0.0 136.9 jit_solution(15960436071740813237)
XLA Ops:
  0.6 1.3 xor_reduce_fusion
  2.6 0.7 and_add_fusion.2
  3.3 0.2 convert_reduce_fusion.2
  3.4 0.1 select_reduce_fusion.1.blocks
  3.6 1.4 and_add_fusion
  4.9 0.1 convert_reduce_fusion.1
  5.0 0.1 select_reduce_fusion.tiles
  5.2 0.0 copy-start
  5.2 1.6 %copy-done = bf16[64,128,128]{2,1,0:T(8,128)(2,1)S(1)} copy-done((bf16[64,128,128]{2,1,0:T(8,128)(2,1)S(1)}, bf16[64,128,128]{2,1,0:T(8,128)(2,1)}, u32[]{:S(2)}) %copy-start) | copy-done | bytes 2097176
  6.8 0.0 copy-start.1
  6.8 0.0 copy-start.2
  6.8 33.9 %gather_tiles.1.whole = bf16[256,128,128]{2,1,0:T(8,128)(2,1)S(1)} custom-call(bf16[64,128,128]{2,1,0:T(8,128)(2,1)S(1)} %copy-done), custom_call_target="tpu_custom_call" | custom-call | tf_op jit(solution)/shard_map/gather_tiles/pallas_call | solution.py:287
  40.7 0.0 copy-done.1
  40.7 0.0 copy-done.2
  40.7 17.5 %layer.1 = (bf16[192,8192]{1,0:T(8,128)(2,1)}, f32[256,128,128]{2,1,0:T(8,128)}) custom-call(s32[64]{0:T(128)S(1)} %select_reduce_fusion.1.blocks, s32[256]{0:T(256)S(1)} %select_reduce_fusion.tiles, s32[256]{0:T(256)S(1)} %fusion.4.places, bf16[192,8192]{1,0:T(8,128)(2,1)S(1)} %copy-done.1, bf16[192,8192]{1,0:T(8,128)(2,1)S(1)} %copy-done.2, ...), custom_call_target="tpu_custom_call" | custom-call | flops 4831838208 | bytes 34603008 | tf_op jit(solution)/shard_map/layer/pallas_call | solution.py:112
  58.2 76.1 %reduce_terms.1 = bf16[8,2,4,1,128,128]{5,4,3,2,1,0:T(8,128)(2,1)S(1)} custom-call(f32[2,8,2,8,128,128]{5,4,3,2,1,0:T(8,128)} %bitcast.4), custom_call_target="tpu_custom_call" | custom-call | tf_op jit(solution)/shard_map/reduce_terms/pallas_call | solution.py:496
  134.2 2.7 %bitcast_convert_fusion = f32[64,128,128]{2,1,0:T(8,128)} fusion(bf16[8,2,4,1,128,128]{5,4,3,2,1,0:T(8,128)(2,1)S(1)} %reduce_terms.1), kind=kLoop, calls=%fused_computation | loop fusion | flops 1048576 | bytes 6291456 | tf_op jit(solution)/shard_map/convert_element_type | solution.py:547
  (2 shorter events, 0.0 us)
Async XLA Ops:
  5.2 1.6 %copy-start = (bf16[64,128,128]{2,1,0:T(8,128)(2,1)S(1)}, bf16[64,128,128]{2,1,0:T(8,128)(2,1)}, u32[]{:S(2)}) copy-start(bf16[64,128,128]{2,1,0:T(8,128)(2,1)} %mine.1) | copy-start | bytes 6291460
  6.8 33.9 %copy-start.1 = (bf16[192,8192]{1,0:T(8,128)(2,1)S(1)}, bf16[192,8192]{1,0:T(8,128)(2,1)}, u32[]{:S(2)}) copy-start(bf16[192,8192]{1,0:T(8,128)(2,1)} %features.1) | copy-start | bytes 9437188
  6.8 33.9 %copy-start.2 = (bf16[192,8192]{1,0:T(8,128)(2,1)S(1)}, bf16[192,8192]{1,0:T(8,128)(2,1)}, u32[]{:S(2)}) copy-start(bf16[192,8192]{1,0:T(8,128)(2,1)} %grads.1) | copy-start | bytes 9437188

commit v5 on v4

--- a/solution.py
+++ b/solution.py
@@ -314,6 +314,7 @@
     terms,
     out,
     own,
+    mail,
     rc,
     sx,
     rx,
@@ -323,6 +324,7 @@
     rz,
     done,
     own_sem,
+    mail_sem,
     cs,
     cr,
     xs,
@@ -352,10 +354,13 @@
         return ref[...].astype(jnp.float32)
 
     def core_copy(p):
-        return remote(terms.at[1 - me.c, p], rc.at[p], cs.at[p], cr.at[p], other)
+        return remote(mail.at[p], rc.at[p], cs.at[p], cr.at[p], other)
 
     def own_copy(p):
         return pltpu.make_async_copy(terms.at[me.c, p], own.at[p], own_sem.at[p])
+
+    def mail_copy(p):
+        return pltpu.make_async_copy(terms.at[1 - me.c, p], mail.at[p], mail_sem.at[p])
 
     def x_copy(p, k):
         return remote(sx.at[p, k - 1], rx.at[p, k - 1], xs.at[p, k - 1], xr.at[p, k - 1], xp[k - 1])
@@ -384,8 +389,8 @@
         core_copy(p).wait_recv()
         if p + WINDOW < pieces:
             core_copy(p).wait_send()
+            mail_copy(p + WINDOW).wait()
             core_copy(p + WINDOW).start()
-            own_copy(p + WINDOW).start()
         for k in range(1, nx):
             x = me.step_x(k)
 
@@ -468,9 +473,12 @@
                 z = me.step_z(-m)
                 spread_y(p, j, m, done.at[p], y, z).wait_recv()
 
+    for p in range(pieces):
+        mail_copy(p).start()
+        own_copy(p).start()
     for p in range(min(WINDOW, pieces)):
+        mail_copy(p).wait()
         core_copy(p).start()
-        own_copy(p).start()
     stages = [over_x, over_y, over_z, finish, pass_on, collect]
     for t in range(pieces + len(stages) - 1):
         for s, stage in enumerate(stages):
@@ -496,9 +504,10 @@
     return pl.pallas_call(
         functools.partial(reduce_kernel, place, pieces, q),
         in_specs=[pl.BlockSpec(memory_space=pl.ANY)],
-        out_specs=pl.BlockSpec(memory_space=pl.ANY),
+        out_specs=pl.BlockSpec(memory_space=pltpu.VMEM),
         out_shape=jax.ShapeDtypeStruct((pieces, ny, nz, q, side, side), jnp.bfloat16),
         scratch_shapes=[
+            room(nx, n, dtype=jnp.float32),
             room(nx, n, dtype=jnp.float32),
             room(nx, n, dtype=jnp.float32),
             room(nx - 1, n),
@@ -508,6 +517,7 @@
             room(nz - 1, q),
             room(nz - 1, q),
             room(q),
+            dma((pieces,)),
             dma((pieces,)),
             dma((pieces,)),
             dma((pieces,)),

time: 137 us -> 138 us (level)
  Pallas kernels: 127 us -> 129 us
where the time goes in v5:
time: 138 us
  Pallas kernels  129 us (93%)
  other arithmetic  6.55 us (5%)
  local copies, waits for them, and re-layouts  1.59 us (1%)
    pallas_call x1, Pallas kernels, reduce_terms(): pl.pallas_call(functools.partial(reduce_kernel, place, pieces, q), in_spe...  77.2 us
    pallas_call x1, Pallas kernels, gather_tiles(): pl.pallas_call(functools.partial(gather_kernel, place, pieces), in_specs=...  33.9 us
    pallas_call x1, Pallas kernels, layer(): pl.pallas_call(functools.partial(layer_kernel, steps), in_specs=[smem] *...  17.5 us

profile of v5, /device:TPU:0, one launch (start us, length us, event | category | flops | bytes accessed | tf_op | source)
XLA Modules:
  0.0 138.1 jit_solution(14374432125373214393)
XLA Ops:
  0.6 1.3 xor_reduce_fusion
  2.6 0.7 and_add_fusion.2
  3.3 0.2 convert_reduce_fusion.2
  3.4 0.1 select_reduce_fusion.1.blocks
  3.6 1.4 and_add_fusion
  4.9 0.1 convert_reduce_fusion.1
  5.0 0.1 select_reduce_fusion.tiles
  5.2 0.0 copy-start
  5.2 1.6 %copy-done = bf16[64,128,128]{2,1,0:T(8,128)(2,1)S(1)} copy-done((bf16[64,128,128]{2,1,0:T(8,128)(2,1)S(1)}, bf16[64,128,128]{2,1,0:T(8,128)(2,1)}, u32[]{:S(2)}) %copy-start) | copy-done | bytes 2097176
  6.8 0.0 copy-start.1
  6.8 0.0 copy-start.2
  6.8 33.9 %gather_tiles.1.whole = bf16[256,128,128]{2,1,0:T(8,128)(2,1)S(1)} custom-call(bf16[64,128,128]{2,1,0:T(8,128)(2,1)S(1)} %copy-done), custom_call_target="tpu_custom_call" | custom-call | tf_op jit(solution)/shard_map/gather_tiles/pallas_call | solution.py:287
  40.7 0.0 copy-done.1
  40.7 0.0 copy-done.2
  40.7 17.5 %layer.1 = (bf16[192,8192]{1,0:T(8,128)(2,1)}, f32[256,128,128]{2,1,0:T(8,128)}) custom-call(s32[64]{0:T(128)S(1)} %select_reduce_fusion.1.blocks, s32[256]{0:T(256)S(1)} %select_reduce_fusion.tiles, s32[256]{0:T(256)S(1)} %fusion.4.places, bf16[192,8192]{1,0:T(8,128)(2,1)S(1)} %copy-done.1, bf16[192,8192]{1,0:T(8,128)(2,1)S(1)} %copy-done.2, ...), custom_call_target="tpu_custom_call" | custom-call | flops 4831838208 | bytes 34603008 | tf_op jit(solution)/shard_map/layer/pallas_call | solution.py:112
  58.2 77.2 %reduce_terms.1 = bf16[8,2,4,1,128,128]{5,4,3,2,1,0:T(8,128)(2,1)S(1)} custom-call(f32[2,8,2,8,128,128]{5,4,3,2,1,0:T(8,128)} %bitcast.4), custom_call_target="tpu_custom_call" | custom-call | tf_op jit(solution)/shard_map/reduce_terms/pallas_call | solution.py:504
  135.4 2.7 %bitcast_convert_fusion = f32[64,128,128]{2,1,0:T(8,128)} fusion(bf16[8,2,4,1,128,128]{5,4,3,2,1,0:T(8,128)(2,1)S(1)} %reduce_terms.1), kind=kLoop, calls=%fused_computation | loop fusion | flops 1048576 | bytes 6291456 | tf_op jit(solution)/shard_map/convert_element_type | solution.py:557
  (2 shorter events, 0.0 us)
Async XLA Ops:
  5.2 1.6 %copy-start = (bf16[64,128,128]{2,1,0:T(8,128)(2,1)S(1)}, bf16[64,128,128]{2,1,0:T(8,128)(2,1)}, u32[]{:S(2)}) copy-start(bf16[64,128,128]{2,1,0:T(8,128)(2,1)} %mine.1) | copy-start | bytes 6291460
  6.8 33.9 %copy-start.1 = (bf16[192,8192]{1,0:T(8,128)(2,1)S(1)}, bf16[192,8192]{1,0:T(8,128)(2,1)}, u32[]{:S(2)}) copy-start(bf16[192,8192]{1,0:T(8,128)(2,1)} %features.1) | copy-start | bytes 9437188
  6.8 33.9 %copy-start.2 = (bf16[192,8192]{1,0:T(8,128)(2,1)S(1)}, bf16[192,8192]{1,0:T(8,128)(2,1)}, u32[]{:S(2)}) copy-start(bf16[192,8192]{1,0:T(8,128)(2,1)} %grads.1) | copy-start | bytes 9437188

commit v6 on v4

--- a/solution.py
+++ b/solution.py
@@ -16,10 +16,8 @@
 
 def gelu_slope(value):
     square = value * value
-    hyper = jnp.tanh(ROOT * (value + 0.044715 * square * value))
-    return 0.5 * (1.0 + hyper) + 0.5 * value * (1.0 - hyper * hyper) * ROOT * (
-        1.0 + 3.0 * 0.044715 * square
-    )
+    half = 0.5 + 0.5 * jnp.tanh(value * (ROOT + (0.044715 * ROOT) * square))
+    return half + half * (1.0 - half) * (value * (2.0 * ROOT + (6.0 * 0.044715 * ROOT) * square))
 
 
 def pattern(tile_row, tile_column, nblocks):
@@ -68,37 +66,40 @@
         back = lax.dot_general(
             slope, weight, (((1,), (1,)), ((), ())), preferred_element_type=jnp.float32
         )
-        result = (grad + back).astype(jnp.bfloat16)
-        for k, at in enumerate(columns):
-            out_ref[:, at] = result[:, k * side : (k + 1) * side]
         term = lax.dot_general(
             feature, slope, (((0,), (0,)), ((), ())), preferred_element_type=jnp.float32
         )
-        for c in range(n):
-            for r in range(n):
-                term_buf[slot, c * n + r] = term[
-                    c * side : (c + 1) * side, r * side : (r + 1) * side
-                ]
-        for k in range(m):
-            pltpu.make_async_copy(
-                term_buf.at[slot, k], partial_ref.at[places[g * m + k]], sems.at[slot]
-            ).start()
+        return columns, (grad + back).astype(jnp.bfloat16), term
 
     slots = term_buf.shape[0]
 
     def body(i, carry):
-        for k in range(slots):
-
-            @pl.when(i > 0)
-            def _():
-                drain(k)
-
-            group(i * slots + k, k)
+        @pl.when(i > 0)
+        def _():
+            for slot in range(slots):
+                drain(slot)
+
+        found = [group(i * slots + slot, slot) for slot in range(slots)]
+        for slot, (columns, result, term) in enumerate(found):
+            for k, at in enumerate(columns):
+                out_ref[:, at] = result[:, k * side : (k + 1) * side]
+            for c in range(n):
+                for r in range(n):
+                    term_buf[slot, c * n + r] = term[
+                        c * side : (c + 1) * side, r * side : (r + 1) * side
+                    ]
+        for slot in range(slots):
+            for k in range(m):
+                pltpu.make_async_copy(
+                    term_buf.at[slot, k],
+                    partial_ref.at[places[(i * slots + slot) * m + k]],
+                    sems.at[slot],
+                ).start()
         return carry
 
     lax.fori_loop(0, steps // slots, body, 0)
-    for k in range(slots):
-        drain(k)
+    for slot in range(slots):
+        drain(slot)
 
 
 def layer(features, grad_out, whole, blocks, tiles, places):
@@ -184,122 +185,146 @@
 
 
 def gather_kernel(
-    place, pieces, mine, whole, own_sem, xs, xr, ys, yr, cs, cr, ws, wr
+    place, nw, pieces, mine, whole, own_sem, xs, xr, ys, yr, zs, zr, ds, dr, cs, cr, ws, wr
 ):
     me = place.locate()
+    nx, ny = me.nx, me.ny
     tiles = mine.shape[0]
-    part = tiles // me.ny
+    part = tiles // (ny * nw)
     q = part // pieces
+    w = me.z % nw
     other = me.at(c=1 - me.c)
     xp, yp = me.x_peers(), me.y_peers()
-    meet(xp + yp + [other])
-
-    def span(x, y, p):
-        return pl.ds((x * 2 + me.c) * tiles + y * part + p * q, q)
-
+    zp = me.at(z=me.z + 1 - 2 * w) if nw == 2 else None
+    meet(xp + yp + [other] + ([zp] if nw == 2 else []))
+    run = ny * nw * q
     started = []
 
     def go(copy):
         copy.start()
         started.append(copy)
 
-    def x_copy(p, k):
+    def inner(y, v, p):
+        return y * (nw * part) + v * part + p * q
+
+    def span(x, y, v, p, core=None):
+        core = me.c if core is None else core
+        return whole.at[pl.ds((x * 2 + core) * tiles + inner(y, v, p), q)]
+
+    def x_copy(p, k, x):
         return remote(
-            mine.at[pl.ds(me.y * part + p * q, q)],
-            whole.at[span(me.x, me.y, p)],
+            mine.at[pl.ds(inner(me.y, w, p), q)],
+            span(x, me.y, w, p),
             xs.at[k - 1, p],
             xr.at[k - 1, p],
             xp[k - 1],
         )
 
     def home(core, p):
-        return pl.ds((me.x * 2 + core) * tiles + p * q * me.ny, q * me.ny)
+        return whole.at[pl.ds((me.x * 2 + core) * tiles + p * run, run)]
 
     def own_copy(p):
-        src = mine.at[pl.ds(p * q * me.ny, q * me.ny)]
-        return pltpu.make_async_copy(src, whole.at[home(me.c, p)], own_sem.at[p])
-
-    def core_copy(p):
-        src = mine.at[pl.ds(p * q * me.ny, q * me.ny)]
-        return remote(src, whole.at[home(me.c, p)], ws.at[p], wr.at[p], other)
-
-    def to_other(x, y, k, j, p):
-        at = whole.at[span(x, y, p)]
-        go(remote(at, at, cs.at[k - 1, j, p], cr.at[k - 1, j, p], other))
-
-    def y_copy(p, k, j, y):
-        at = whole.at[span(me.step_x(-k), y, p)]
+        return pltpu.make_async_copy(mine.at[pl.ds(p * run, run)], home(me.c, p), own_sem.at[p])
+
+    def core_copy(p, core):
+        return remote(mine.at[pl.ds(p * run, run)], home(core, p), ws.at[p], wr.at[p], other)
+
+    def in_chip(k, j, v, p, at):
+        return remote(at, at, cs.at[k - 1, j, v, p], cr.at[k - 1, j, v, p], other)
+
+    def y_copy(k, j, y, p):
+        at = span(me.step_x(-k), y, w, p)
         return remote(at, at, ys.at[k - 1, j - 1, p], yr.at[k - 1, j - 1, p], yp[j - 1])
 
+    def z_copy(k, v, p):
+        at = span(me.step_x(-k), me.y, v, p)
+        return remote(at, at, zs.at[k - 1, p], zr.at[k - 1, p], zp)
+
+    def last_copy(k, j, y, v, p):
+        at = span(me.step_x(-k), y, v, p)
+        peer = zp if p % 2 == 0 else yp[j - 1]
+        return remote(at, at, ds.at[k - 1, j - 1, p], dr.at[k - 1, j - 1, p], peer)
+
     def land_x(p):
-        for k in range(1, me.nx):
+        for k in range(1, nx):
             x = me.step_x(-k)
-            x_copy(p, k).wait_send()
-            remote(
-                mine.at[pl.ds(0, q)], whole.at[span(x, me.y, p)], xs.at[k - 1, p], xr.at[k - 1, p], xp[k - 1]
-            ).wait_recv()
+            x_copy(p, k, x).wait_recv()
+            for j in range(1, ny):
+                go(y_copy(k, j, me.y, p))
+            if nw == 2:
+                go(z_copy(k, w, p))
+            go(in_chip(k, 0, 0, p, span(x, me.y, w, p)))
+            x_copy(p, k, me.x).wait_send()
             if p + WINDOW < pieces:
-                x_copy(p + WINDOW, k).start()
-            for j in range(1, me.ny):
-                go(y_copy(p, k, j, me.y))
-            to_other(x, me.y, k, 0, p)
-        go(core_copy(p))
+                x_copy(p + WINDOW, k, me.x).start()
+        go(core_copy(p, me.c))
         own_copy(p).start()
 
-    def land_y(p):
-        for k in range(1, me.nx):
+    def land_yz(p):
+        for k in range(1, nx):
             x = me.step_x(-k)
-            for j in range(1, me.ny):
+            for j in range(1, ny):
                 y = me.step_y(-j)
-                y_copy(p, k, j, y).wait_recv()
-                to_other(x, y, k, j, p)
+                y_copy(k, j, y, p).wait_recv()
+                if nw == 2 and p % 2 == 0:
+                    go(last_copy(k, j, y, w, p))
+                go(in_chip(k, j, 0, p, span(x, y, w, p)))
+            if nw == 2:
+                z_copy(k, 1 - w, p).wait_recv()
+                if p % 2 == 1:
+                    for j in range(1, ny):
+                        go(last_copy(k, j, me.y, 1 - w, p))
+                go(in_chip(k, 0, 1, p, span(x, me.y, 1 - w, p)))
+
+    def land_last(p):
+        for k in range(1, nx):
+            x = me.step_x(-k)
+            for j in range(1, ny):
+                y = me.step_y(-j)
+                last_copy(k, j, y, 1 - w, p).wait_recv()
+                go(in_chip(k, j, 1, p, span(x, y, 1 - w, p)))
 
     for p in range(min(WINDOW, pieces)):
-        for k in range(1, me.nx):
-            x_copy(p, k).start()
-    for t in range(pieces + 1):
-        if t < pieces:
-            land_x(t)
-        if t >= 1:
-            land_y(t - 1)
+        for k in range(1, nx):
+            x_copy(p, k, me.x).start()
+    stages = [land_x, land_yz] + ([land_last] if nw == 2 else [])
+    for t in range(pieces + len(stages) - 1):
+        for s, stage in enumerate(stages):
+            if 0 <= t - s < pieces:
+                stage(t - s)
     for p in range(pieces):
         own_copy(p).wait()
-        away = whole.at[home(1 - me.c, p)]
-        remote(away, away, ws.at[p], wr.at[p], other).wait_recv()
-        for k in range(1, me.nx):
+        core_copy(p, 1 - me.c).wait_recv()
+        for k in range(1, nx):
             x = me.step_x(-k)
-            for j in range(me.ny):
+            for j in range(ny):
                 y = me.step_y(-j)
-                at = whole.at[
-                    pl.ds((x * 2 + 1 - me.c) * tiles + y * part + p * q, q)
-                ]
-                remote(at, at, cs.at[k - 1, j, p], cr.at[k - 1, j, p], other).wait_recv()
+                for v in range(nw):
+                    u = w if v == 0 else 1 - w
+                    in_chip(k, j, v, p, span(x, y, u, p, 1 - me.c)).wait_recv()
     for copy in started:
         copy.wait_send()
 
 
 def gather_tiles(mine, place):
     tiles, side, _ = mine.shape
-    part = tiles // place.ny
-    pieces = 8 if part % 8 == 0 else 1
     nx, ny = place.nx, place.ny
+    nw = 2 if place.nz % 2 == 0 and tiles % (2 * ny) == 0 else 1
+    part = tiles // (ny * nw)
+    pieces = 4 if part % 4 == 0 else 1
     dma = pltpu.SemaphoreType.DMA
     return pl.pallas_call(
-        functools.partial(gather_kernel, place, pieces),
+        functools.partial(gather_kernel, place, nw, pieces),
         in_specs=[pl.BlockSpec(memory_space=pltpu.VMEM)],
         out_specs=pl.BlockSpec(memory_space=pltpu.VMEM),
         out_shape=jax.ShapeDtypeStruct((tiles * nx * 2, side, side), mine.dtype),
-        scratch_shapes=[
-            dma((pieces,)),
-            dma((nx - 1, pieces)),
-            dma((nx - 1, pieces)),
-            dma((nx - 1, ny - 1, pieces)),
-            dma((nx - 1, ny - 1, pieces)),
-            dma((nx - 1, ny, pieces)),
-            dma((nx - 1, ny, pieces)),
-            dma((pieces,)),
-            dma((pieces,)),
-        ],
+        scratch_shapes=[dma((pieces,))]
+        + [dma((nx - 1, pieces))] * 2
+        + [dma((nx - 1, ny - 1, pieces))] * 2
+        + [dma((nx - 1, pieces))] * 2
+        + [dma((nx - 1, ny - 1, pieces))] * 2
+        + [dma((nx - 1, ny, nw, pieces))] * 2
+        + [dma((pieces,))] * 2,
         compiler_params=pltpu.CompilerParams(
             collective_id=1, has_side_effects=True, vmem_limit_bytes=24 * 2**20
         ),

time: 137 us -> 139 us (1.015)
  Pallas kernels: 127 us -> 129 us
    pallas_call x1, Pallas kernels: 17.5 us -> 24 us  [layer(): pl.pallas_call(functools.partial(layer_kernel, steps), in_specs=[smem] *...]
    pallas_call x1, Pallas kernels: 33.9 us -> 31.1 us  [gather_tiles(): pl.pallas_call(functools.partial(gather_kernel, place, nw, pieces), in_sp...]
    pallas_call x1, Pallas kernels: 76.1 us -> 74.1 us  [reduce_terms(): pl.pallas_call(functools.partial(reduce_kernel, place, pieces, q), in_spe...]
where the time goes in v6:
time: 139 us
  Pallas kernels  129 us (93%)
  other arithmetic  6.55 us (5%)
  local copies, waits for them, and re-layouts  1.59 us (1%)
    pallas_call x1, Pallas kernels, reduce_terms(): pl.pallas_call(functools.partial(reduce_kernel, place, pieces, q), in_spe...  74.1 us
    pallas_call x1, Pallas kernels, gather_tiles(): pl.pallas_call(functools.partial(gather_kernel, place, nw, pieces), in_sp...  31.1 us
    pallas_call x1, Pallas kernels, layer(): pl.pallas_call(functools.partial(layer_kernel, steps), in_specs=[smem] *...  24 us

profile of v6, /device:TPU:0, one launch (start us, length us, event | category | flops | bytes accessed | tf_op | source)
XLA Modules:
  0.0 138.7 jit_solution(16466996079769029103)
XLA Ops:
  0.6 1.3 xor_reduce_fusion
  2.6 0.7 and_add_fusion.2
  3.3 0.2 convert_reduce_fusion.2
  3.4 0.1 select_reduce_fusion.1.blocks
  3.6 1.4 and_add_fusion
  4.9 0.1 convert_reduce_fusion.1
  5.0 0.1 select_reduce_fusion.tiles
  5.2 0.0 copy-start
  5.2 1.6 %copy-done = bf16[64,128,128]{2,1,0:T(8,128)(2,1)S(1)} copy-done((bf16[64,128,128]{2,1,0:T(8,128)(2,1)S(1)}, bf16[64,128,128]{2,1,0:T(8,128)(2,1)}, u32[]{:S(2)}) %copy-start) | copy-done | bytes 2097176
  6.8 0.0 copy-start.1
  6.8 0.0 copy-start.2
  6.8 31.1 %gather_tiles.1.whole = bf16[256,128,128]{2,1,0:T(8,128)(2,1)S(1)} custom-call(bf16[64,128,128]{2,1,0:T(8,128)(2,1)S(1)} %copy-done), custom_call_target="tpu_custom_call" | custom-call | tf_op jit(solution)/shard_map/gather_tiles/pallas_call | solution.py:316
  37.9 0.0 copy-done.1
  37.9 0.0 copy-done.2
  37.9 24.0 %layer.1 = (bf16[192,8192]{1,0:T(8,128)(2,1)}, f32[256,128,128]{2,1,0:T(8,128)}) custom-call(s32[64]{0:T(128)S(1)} %select_reduce_fusion.1.blocks, s32[256]{0:T(256)S(1)} %select_reduce_fusion.tiles, s32[256]{0:T(256)S(1)} %fusion.4.places, bf16[192,8192]{1,0:T(8,128)(2,1)S(1)} %copy-done.1, bf16[192,8192]{1,0:T(8,128)(2,1)S(1)} %copy-done.2, ...), custom_call_target="tpu_custom_call" | custom-call | flops 4831838208 | bytes 34603008 | tf_op jit(solution)/shard_map/layer/pallas_call | solution.py:113
  61.9 74.1 %reduce_terms.1 = bf16[8,2,4,1,128,128]{5,4,3,2,1,0:T(8,128)(2,1)S(1)} custom-call(f32[2,8,2,8,128,128]{5,4,3,2,1,0:T(8,128)} %bitcast.4), custom_call_target="tpu_custom_call" | custom-call | tf_op jit(solution)/shard_map/reduce_terms/pallas_call | solution.py:521
  136.0 2.7 %bitcast_convert_fusion = f32[64,128,128]{2,1,0:T(8,128)} fusion(bf16[8,2,4,1,128,128]{5,4,3,2,1,0:T(8,128)(2,1)S(1)} %reduce_terms.1), kind=kLoop, calls=%fused_computation | loop fusion | flops 1048576 | bytes 6291456 | tf_op jit(solution)/shard_map/convert_element_type | solution.py:572
  (2 shorter events, 0.0 us)
Async XLA Ops:
  5.2 1.6 %copy-start = (bf16[64,128,128]{2,1,0:T(8,128)(2,1)S(1)}, bf16[64,128,128]{2,1,0:T(8,128)(2,1)}, u32[]{:S(2)}) copy-start(bf16[64,128,128]{2,1,0:T(8,128)(2,1)} %mine.1) | copy-start | bytes 6291460
  6.8 31.1 %copy-start.1 = (bf16[192,8192]{1,0:T(8,128)(2,1)S(1)}, bf16[192,8192]{1,0:T(8,128)(2,1)}, u32[]{:S(2)}) copy-start(bf16[192,8192]{1,0:T(8,128)(2,1)} %features.1) | copy-start | bytes 9437188
  6.8 31.1 %copy-start.2 = (bf16[192,8192]{1,0:T(8,128)(2,1)S(1)}, bf16[192,8192]{1,0:T(8,128)(2,1)}, u32[]{:S(2)}) copy-start(bf16[192,8192]{1,0:T(8,128)(2,1)} %grads.1) | copy-start | bytes 9437188

commit v7 on v6

--- a/solution.py
+++ b/solution.py
@@ -66,40 +66,37 @@
         back = lax.dot_general(
             slope, weight, (((1,), (1,)), ((), ())), preferred_element_type=jnp.float32
         )
+        result = (grad + back).astype(jnp.bfloat16)
+        for k, at in enumerate(columns):
+            out_ref[:, at] = result[:, k * side : (k + 1) * side]
         term = lax.dot_general(
             feature, slope, (((0,), (0,)), ((), ())), preferred_element_type=jnp.float32
         )
-        return columns, (grad + back).astype(jnp.bfloat16), term
+        for c in range(n):
+            for r in range(n):
+                term_buf[slot, c * n + r] = term[
+                    c * side : (c + 1) * side, r * side : (r + 1) * side
+                ]
+        for k in range(m):
+            pltpu.make_async_copy(
+                term_buf.at[slot, k], partial_ref.at[places[g * m + k]], sems.at[slot]
+            ).start()
 
     slots = term_buf.shape[0]
 
     def body(i, carry):
-        @pl.when(i > 0)
-        def _():
-            for slot in range(slots):
-                drain(slot)
-
-        found = [group(i * slots + slot, slot) for slot in range(slots)]
-        for slot, (columns, result, term) in enumerate(found):
-            for k, at in enumerate(columns):
-                out_ref[:, at] = result[:, k * side : (k + 1) * side]
-            for c in range(n):
-                for r in range(n):
-                    term_buf[slot, c * n + r] = term[
-                        c * side : (c + 1) * side, r * side : (r + 1) * side
-                    ]
-        for slot in range(slots):
-            for k in range(m):
-                pltpu.make_async_copy(
-                    term_buf.at[slot, k],
-                    partial_ref.at[places[(i * slots + slot) * m + k]],
-                    sems.at[slot],
-                ).start()
+        for k in range(slots):
+
+            @pl.when(i > 0)
+            def _():
+                drain(k)
+
+            group(i * slots + k, k)
         return carry
 
     lax.fori_loop(0, steps // slots, body, 0)
-    for slot in range(slots):
-        drain(slot)
+    for k in range(slots):
+        drain(k)
 
 
 def layer(features, grad_out, whole, blocks, tiles, places):
@@ -339,6 +336,8 @@
     terms,
     out,
     own,
+    mail,
+    sc,
     rc,
     sx,
     rx,
@@ -348,6 +347,7 @@
     rz,
     done,
     own_sem,
+    mail_sem,
     cs,
     cr,
     xs,
@@ -377,10 +377,13 @@
         return ref[...].astype(jnp.float32)
 
     def core_copy(p):
-        return remote(terms.at[1 - me.c, p], rc.at[p], cs.at[p], cr.at[p], other)
+        return remote(sc.at[p], rc.at[p], cs.at[p], cr.at[p], other)
 
     def own_copy(p):
         return pltpu.make_async_copy(terms.at[me.c, p], own.at[p], own_sem.at[p])
+
+    def mail_copy(p):
+        return pltpu.make_async_copy(terms.at[1 - me.c, p], mail.at[p], mail_sem.at[p])
 
     def x_copy(p, k):
         return remote(sx.at[p, k - 1], rx.at[p, k - 1], xs.at[p, k - 1], xr.at[p, k - 1], xp[k - 1])
@@ -404,13 +407,26 @@
     def keep_copy(p):
         return pltpu.make_async_copy(done.at[p], out.at[p, me.y, me.z], keep_sem.at[p])
 
+    def fetch(p):
+        if p < pieces:
+            mail_copy(p).start()
+            own_copy(p).start()
+
+    def post(p):
+        if p < pieces:
+            mail_copy(p).wait()
+
+            def body(n, carry):
+                for x in range(nx):
+                    sc[p, x, n] = mail[p, x, n].astype(jnp.bfloat16)
+                return carry
+
+            lax.fori_loop(0, ny * nz * q, body, 0)
+            go(core_copy(p))
+
     def over_x(p):
         own_copy(p).wait()
         core_copy(p).wait_recv()
-        if p + WINDOW < pieces:
-            core_copy(p).wait_send()
-            core_copy(p + WINDOW).start()
-            own_copy(p + WINDOW).start()
         for k in range(1, nx):
             x = me.step_x(k)
 
@@ -421,6 +437,8 @@
 
             lax.fori_loop(0, ny * nz * q, body, 0)
             go(x_copy(p, k))
+        post(p + WINDOW)
+        fetch(p + WINDOW + 1)
 
     def up_to_x(p, n):
         total = wide(own.at[p, me.x, n]) + wide(rc.at[p, me.x, n])
@@ -493,9 +511,10 @@
                 z = me.step_z(-m)
                 spread_y(p, j, m, done.at[p], y, z).wait_recv()
 
-    for p in range(min(WINDOW, pieces)):
-        core_copy(p).start()
-        own_copy(p).start()
+    for p in range(WINDOW + 1):
+        fetch(p)
+    for p in range(WINDOW):
+        post(p)
     stages = [over_x, over_y, over_z, finish, pass_on, collect]
     for t in range(pieces + len(stages) - 1):
         for s, stage in enumerate(stages):
@@ -503,8 +522,6 @@
                 stage(t - s)
     for p in range(pieces):
         keep_copy(p).wait()
-        if p + WINDOW >= pieces:
-            core_copy(p).wait_send()
     for copy in started:
         copy.wait_send()
 
@@ -521,11 +538,13 @@
     return pl.pallas_call(
         functools.partial(reduce_kernel, place, pieces, q),
         in_specs=[pl.BlockSpec(memory_space=pl.ANY)],
-        out_specs=pl.BlockSpec(memory_space=pl.ANY),
+        out_specs=pl.BlockSpec(memory_space=pltpu.VMEM),
         out_shape=jax.ShapeDtypeStruct((pieces, ny, nz, q, side, side), jnp.bfloat16),
         scratch_shapes=[
             room(nx, n, dtype=jnp.float32),
             room(nx, n, dtype=jnp.float32),
+            room(nx, n),
+            room(nx, n),
             room(nx - 1, n),
             room(nx - 1, n),
             room(ny - 1, nz * q),
@@ -533,6 +552,7 @@
             room(nz - 1, q),
             room(nz - 1, q),
             room(q),
+            dma((pieces,)),
             dma((pieces,)),
             dma((pieces,)),
             dma((pieces,)),

time: 139 us -> 133 us (0.957)
  Pallas kernels: 129 us -> 123 us
    pallas_call x1, Pallas kernels: 24 us -> 17.3 us  [layer(): pl.pallas_call(functools.partial(layer_kernel, steps), in_specs=[smem] *...]
where the time goes in v7:
time: 133 us; the launch traced here: 132 us
  Pallas kernels  123 us (92%)
  other arithmetic  6.55 us (5%)
  local copies, waits for them, and re-layouts  1.59 us (1%)
  between operations  1.36 us (1%)
    pallas_call x1, Pallas kernels, reduce_terms(): pl.pallas_call(functools.partial(reduce_kernel, place, pieces, q), in_spe...  74.6 us
    pallas_call x1, Pallas kernels, gather_tiles(): pl.pallas_call(functools.partial(gather_kernel, place, nw, pieces), in_sp...  31.1 us
    pallas_call x1, Pallas kernels, layer(): pl.pallas_call(functools.partial(layer_kernel, steps), in_specs=[smem] *...  17.3 us
    convert_element_type x1, other arithmetic, on_device(): tile_update.reshape(tiles_here, side, side).astype(jnp.float32)  2.68 us

profile of v7, /device:TPU:0, one launch (start us, length us, event | category | flops | bytes accessed | tf_op | source)
XLA Modules:
  0.0 132.5 jit_solution(9735320532800452812)
XLA Ops:
  0.6 1.3 %xor_reduce_fusion = s32[]{:T(128)} fusion(s32[256]{0:T(256)} %param.8, s32[256]{0:T(256)} %param.9), kind=kLoop, calls=%fused_computation.34 | loop fusion | flops 511 | bytes 2052 | tf_op jit(solution)/shard_map/reduce_max | solution.py:25
  2.6 0.7 and_add_fusion.2
  3.3 0.2 convert_reduce_fusion.2
  3.4 0.1 select_reduce_fusion.1.blocks
  3.6 1.4 %and_add_fusion = (s32[256]{0:T(256)S(1)}, s32[256]{0:T(256)S(1)}) fusion(s32[256]{0:T(256)} %param.8, s32[]{:T(128)} %xor_reduce_fusion, s32[]{:T(128)S(6)} %not.2, s32[256]{0:T(256)} %param.9), kind=kLoop, calls=%fused_computation.32 | loop fusion | flops 2048 | bytes 4104 | tf_op jit(solution)/shard_map/add | solution.py:30
  4.9 0.1 convert_reduce_fusion.1
  5.0 0.1 select_reduce_fusion.tiles
  5.2 0.0 copy-start
  5.2 1.6 %copy-done = bf16[64,128,128]{2,1,0:T(8,128)(2,1)S(1)} copy-done((bf16[64,128,128]{2,1,0:T(8,128)(2,1)S(1)}, bf16[64,128,128]{2,1,0:T(8,128)(2,1)}, u32[]{:S(2)}) %copy-start) | copy-done | bytes 2097176
  6.8 0.0 copy-start.1
  6.8 0.0 copy-start.2
  6.8 31.1 %gather_tiles.1.whole = bf16[256,128,128]{2,1,0:T(8,128)(2,1)S(1)} custom-call(bf16[64,128,128]{2,1,0:T(8,128)(2,1)S(1)} %copy-done), custom_call_target="tpu_custom_call" | custom-call | tf_op jit(solution)/shard_map/gather_tiles/pallas_call | solution.py:313
  37.9 0.0 copy-done.1
  37.9 0.0 copy-done.2
  37.9 17.3 %layer.1 = (bf16[192,8192]{1,0:T(8,128)(2,1)}, f32[256,128,128]{2,1,0:T(8,128)}) custom-call(s32[64]{0:T(128)S(1)} %select_reduce_fusion.1.blocks, s32[256]{0:T(256)S(1)} %select_reduce_fusion.tiles, s32[256]{0:T(256)S(1)} %fusion.4.places, bf16[192,8192]{1,0:T(8,128)(2,1)S(1)} %copy-done.1, bf16[192,8192]{1,0:T(8,128)(2,1)S(1)} %copy-done.2, ...), custom_call_target="tpu_custom_call" | custom-call | flops 4831838208 | bytes 34603008 | tf_op jit(solution)/shard_map/layer/pallas_call | solution.py:110
  55.2 74.6 %reduce_terms.1 = bf16[8,2,4,1,128,128]{5,4,3,2,1,0:T(8,128)(2,1)S(1)} custom-call(f32[2,8,2,8,128,128]{5,4,3,2,1,0:T(8,128)} %bitcast.4), custom_call_target="tpu_custom_call" | custom-call | tf_op jit(solution)/shard_map/reduce_terms/pallas_call | solution.py:538
  129.8 2.7 %bitcast_convert_fusion = f32[64,128,128]{2,1,0:T(8,128)} fusion(bf16[8,2,4,1,128,128]{5,4,3,2,1,0:T(8,128)(2,1)S(1)} %reduce_terms.1), kind=kLoop, calls=%fused_computation | loop fusion | flops 1048576 | bytes 6291456 | tf_op jit(solution)/shard_map/convert_element_type | solution.py:592
  (2 shorter events, 0.0 us)
Async XLA Ops:
  5.2 1.6 %copy-start = (bf16[64,128,128]{2,1,0:T(8,128)(2,1)S(1)}, bf16[64,128,128]{2,1,0:T(8,128)(2,1)}, u32[]{:S(2)}) copy-start(bf16[64,128,128]{2,1,0:T(8,128)(2,1)} %mine.1) | copy-start | bytes 6291460
  6.8 31.1 %copy-start.1 = (bf16[192,8192]{1,0:T(8,128)(2,1)S(1)}, bf16[192,8192]{1,0:T(8,128)(2,1)}, u32[]{:S(2)}) copy-start(bf16[192,8192]{1,0:T(8,128)(2,1)} %features.1) | copy-start | bytes 9437188
  6.8 31.1 %copy-start.2 = (bf16[192,8192]{1,0:T(8,128)(2,1)S(1)}, bf16[192,8192]{1,0:T(8,128)(2,1)}, u32[]{:S(2)}) copy-start(bf16[192,8192]{1,0:T(8,128)(2,1)} %grads.1) | copy-start | bytes 9437188

commit v8 on v7

--- a/solution.py
+++ b/solution.py
@@ -20,23 +20,41 @@
     return half + half * (1.0 - half) * (value * (2.0 * ROOT + (6.0 * 0.044715 * ROOT) * square))
 
 
-def pattern(tile_row, tile_column, nblocks):
-    total = tile_row.shape[0]
-    mask = jnp.max(jnp.bitwise_xor(tile_row, tile_column))
-    ids = jnp.arange(nblocks, dtype=jnp.int32)
-    keys = jnp.bitwise_and(ids, ~mask) * nblocks + jnp.bitwise_and(ids, mask)
+def pattern(tile_row, tile_column, nblocks, tiles_here, run, nx):
+    total = tile_row.shape[1]
+    f32, i32 = jnp.float32, jnp.int32
+    mask = jnp.max(jnp.bitwise_xor(tile_row, tile_column).astype(f32), axis=1, keepdims=True)
+    mask = mask.astype(i32)
+
+    def key(block):
+        inside = jnp.bitwise_and(block, jnp.broadcast_to(mask, block.shape))
+        return ((block - inside) * nblocks + inside).astype(f32)
 
     def place(block):
-        key = jnp.bitwise_and(block, ~mask) * nblocks + jnp.bitwise_and(block, mask)
-        return jnp.sum((keys[None, :] < key[:, None]).astype(jnp.int32), axis=1)
-
-    places = place(ids)
-    blocks = jnp.sum(jnp.where(places[None, :] == ids[:, None], ids[None, :], 0), axis=1)
+        count = block.shape[1]
+        keys = key(lax.broadcasted_iota(i32, (nblocks, count), 0))
+        below = jnp.where(keys < key(block), 1.0, 0.0)
+        return jnp.sum(below, axis=0, keepdims=True)
+
+    def inverse(values):
+        count = values.shape[1]
+        down = lax.broadcasted_iota(i32, (count, count), 0).astype(f32)
+        along = lax.broadcasted_iota(i32, (count, count), 1).astype(f32)
+        column = jnp.sum(jnp.where(down == along, values, 0.0), axis=1, keepdims=True)
+        return jnp.sum(jnp.where(column == along, down, 0.0), axis=0, keepdims=True)
+
+    def divide(value, by):
+        whole = jnp.floor((value + 0.5) * (1.0 / by))
+        return whole, value - whole * by
+
+    blocks = inverse(place(lax.broadcasted_iota(i32, (1, nblocks), 1)))
     at_row, at_column = place(tile_row), place(tile_column)
-    slots = at_column * SIDE_BLOCKS + at_row % SIDE_BLOCKS
-    every = jnp.arange(total, dtype=jnp.int32)
-    tiles = jnp.sum(jnp.where(slots[None, :] == every[:, None], every[None, :], 0), axis=1)
-    return blocks, tiles
+    tiles = inverse(at_column * SIDE_BLOCKS + divide(at_row, SIDE_BLOCKS)[1])
+    owner, rest = divide(tiles, tiles_here)
+    x, core = divide(owner, 2)
+    piece, left = divide(rest, run)
+    places = ((core * (tiles_here // run) + piece) * nx + x) * run + left
+    return blocks.astype(i32), tiles.astype(i32), places.astype(i32)
 
 
 def layer_kernel(steps, blocks, tiles, places, features, grads, whole, out_ref, partial_ref, term_buf, sems):
@@ -50,13 +68,13 @@
 
     def group(g, slot):
         columns = [
-            pl.ds(pl.multiple_of(blocks[g * n + k] * side, side), side) for k in range(n)
+            pl.ds(pl.multiple_of(blocks[0, g * n + k] * side, side), side) for k in range(n)
         ]
         feature = jnp.concatenate([features[:, at] for at in columns], axis=1)
         grad = jnp.concatenate([grads[:, at] for at in columns], axis=1).astype(jnp.float32)
         weight = jnp.concatenate(
             [
-                jnp.concatenate([whole[tiles[g * m + c * n + r]] for r in range(n)], axis=1)
+                jnp.concatenate([whole[tiles[0, g * m + c * n + r]] for r in range(n)], axis=1)
                 for c in range(n)
             ],
             axis=0,
@@ -79,7 +97,7 @@
                 ]
         for k in range(m):
             pltpu.make_async_copy(
-                term_buf.at[slot, k], partial_ref.at[places[g * m + k]], sems.at[slot]
+                term_buf.at[slot, k], partial_ref.at[places[0, g * m + k]], sems.at[slot]
             ).start()
 
     slots = term_buf.shape[0]
@@ -182,7 +200,8 @@
 
 
 def gather_kernel(
-    place, nw, pieces, mine, whole, own_sem, xs, xr, ys, yr, zs, zr, ds, dr, cs, cr, ws, wr
+    place, nw, pieces, find, mine, row, column, whole, blocks, order, places,
+    own_sem, xs, xr, ys, yr, zs, zr, ds, dr, cs, cr, ws, wr
 ):
     me = place.locate()
     nx, ny = me.nx, me.ny
@@ -284,6 +303,7 @@
     for p in range(min(WINDOW, pieces)):
         for k in range(1, nx):
             x_copy(p, k, me.x).start()
+    blocks[...], order[...], places[...] = find(row[...], column[...])
     stages = [land_x, land_yz] + ([land_last] if nw == 2 else [])
     for t in range(pieces + len(stages) - 1):
         for s, stage in enumerate(stages):
@@ -303,18 +323,26 @@
         copy.wait_send()
 
 
-def gather_tiles(mine, place):
+def gather_tiles(mine, tile_row, tile_column, nblocks, run, place):
     tiles, side, _ = mine.shape
     nx, ny = place.nx, place.ny
     nw = 2 if place.nz % 2 == 0 and tiles % (2 * ny) == 0 else 1
     part = tiles // (ny * nw)
     pieces = 4 if part % 4 == 0 else 1
+    total = tiles * nx * 2
+    find = functools.partial(pattern, nblocks=nblocks, tiles_here=tiles, run=run, nx=nx)
+    vmem = pl.BlockSpec(memory_space=pltpu.VMEM)
     dma = pltpu.SemaphoreType.DMA
     return pl.pallas_call(
-        functools.partial(gather_kernel, place, nw, pieces),
-        in_specs=[pl.BlockSpec(memory_space=pltpu.VMEM)],
-        out_specs=pl.BlockSpec(memory_space=pltpu.VMEM),
-        out_shape=jax.ShapeDtypeStruct((tiles * nx * 2, side, side), mine.dtype),
+        functools.partial(gather_kernel, place, nw, pieces, find),
+        in_specs=[vmem] * 3,
+        out_specs=[vmem] * 4,
+        out_shape=[
+            jax.ShapeDtypeStruct((total, side, side), mine.dtype),
+            jax.ShapeDtypeStruct((1, nblocks), jnp.int32),
+            jax.ShapeDtypeStruct((1, total), jnp.int32),
+            jax.ShapeDtypeStruct((1, total), jnp.int32),
+        ],
         scratch_shapes=[dma((pieces,))]
         + [dma((nx - 1, pieces))] * 2
         + [dma((nx - 1, ny - 1, pieces))] * 2
@@ -326,7 +354,7 @@
             collective_id=1, has_side_effects=True, vmem_limit_bytes=24 * 2**20
         ),
         name="gather_tiles",
-    )(mine)
+    )(mine, tile_row.reshape(1, total), tile_column.reshape(1, total))
 
 
 def reduce_kernel(
@@ -516,10 +544,11 @@
     for p in range(WINDOW):
         post(p)
     stages = [over_x, over_y, over_z, finish, pass_on, collect]
-    for t in range(pieces + len(stages) - 1):
-        for s, stage in enumerate(stages):
-            if 0 <= t - s < pieces:
-                stage(t - s)
+    lags = [0] + list(range(2, len(stages) + 1))
+    for t in range(pieces + lags[-1]):
+        for lag, stage in zip(lags, stages):
+            if 0 <= t - lag < pieces:
+                stage(t - lag)
     for p in range(pieces):
         keep_copy(p).wait()
     for copy in started:
@@ -582,10 +611,9 @@
     nx, n = place.nx, place.ny * place.nz
     pieces = max(count for count in (1, 2, 4, 8) if tiles_here % (n * count) == 0)
     n = tiles_here // pieces
-    blocks, tiles = pattern(tile_row, tile_column, nblocks)
-    owner, rest = tiles // tiles_here, tiles % tiles_here
-    places = ((owner % 2 * pieces + rest // n) * nx + owner // 2) * n + rest % n
-    whole = gather_tiles(weight_tiles, place)
+    whole, blocks, tiles, places = gather_tiles(
+        weight_tiles, tile_row, tile_column, nblocks, n, place
+    )
     grad_features, partial = layer(features, grad_out, whole, blocks, tiles, places)
     terms = partial.reshape(2, pieces, nx, n, side, side)
     tile_update = reduce_terms(terms, place, pieces, n // (place.ny * place.nz))

time: 133 us -> 134 us (level)
  local copies, waits for them, and re-layouts: 1.59 us -> 6.71 us
  other arithmetic: 6.55 us -> 2.68 us
    unnamed x6 -> x10, local copies, waits for them, and re-layouts: 1.59 us -> 6.71 us
    add x4 -> x0, other arithmetic: 2.04 us -> none  [the longest x1 1.36 us: place(): key = jnp.bitwise_and(block, ~mask) * nblocks + jnp.bitwise_and(block, mask)]
where the time goes in v8:
time: 134 us; the launch traced here: 133 us
  Pallas kernels  123 us (92%)
  local copies, waits for them, and re-layouts  6.71 us (5%)
  other arithmetic  2.68 us (2%)
    pallas_call x1, Pallas kernels, reduce_terms(): pl.pallas_call(functools.partial(reduce_kernel, place, pieces, q), in_spe...  74.6 us
    pallas_call x1, Pallas kernels, gather_tiles(): pl.pallas_call(functools.partial(gather_kernel, place, nw, pieces, find),...  31.1 us
    pallas_call x1, Pallas kernels, layer(): pl.pallas_call(functools.partial(layer_kernel, steps), in_specs=[smem] *...  17.5 us
    unnamed x10, local copies, waits for them, and re-layouts  6.71 us

profile of v8, /device:TPU:0, one launch (start us, length us, event | category | flops | bytes accessed | tf_op | source)
XLA Modules:
  0.0 133.2 jit_solution(4912836763570738292)
XLA Ops:
  0.6 0.0 copy-start
  0.6 1.6 %copy-done = bf16[64,128,128]{2,1,0:T(8,128)(2,1)S(1)} copy-done((bf16[64,128,128]{2,1,0:T(8,128)(2,1)S(1)}, bf16[64,128,128]{2,1,0:T(8,128)(2,1)}, u32[]{:S(2)}) %copy-start) | copy-done | bytes 2097176
  2.2 0.0 copy-start.1
  2.2 0.7 copy-done.1
  2.9 0.0 copy-start.2
  2.9 0.7 copy-done.2
  3.6 31.1 %gather_tiles.1 = (bf16[256,128,128]{2,1,0:T(8,128)(2,1)S(1)}, s32[1,64]{1,0:T(1,128)S(1)}, s32[1,256]{1,0:T(1,128)S(1)}, s32[1,256]{1,0:T(1,128)S(1)}) custom-call(bf16[64,128,128]{2,1,0:T(8,128)(2,1)S(1)} %copy-done, s32[1,256]{1,0:T(1,128)S(1)} %bitcast.6, s32[1,256]{1,0:T(1,128)S(1)} %bitcast.7), custom_call_target="tpu_custom_call" | custom-call | tf_op jit(solution)/shard_map/gather_tiles/pallas_call | solution.py:336
  34.7 0.0 copy-start.3
  34.7 1.9 %copy-done.3 = bf16[192,8192]{1,0:T(8,128)(2,1)S(1)} copy-done((bf16[192,8192]{1,0:T(8,128)(2,1)S(1)}, bf16[192,8192]{1,0:T(8,128)(2,1)}, u32[]{:S(2)}) %copy-start.3) | copy-done | bytes 3145752
  36.5 0.0 copy-start.4
  36.5 1.9 %copy-done.4 = bf16[192,8192]{1,0:T(8,128)(2,1)S(1)} copy-done((bf16[192,8192]{1,0:T(8,128)(2,1)S(1)}, bf16[192,8192]{1,0:T(8,128)(2,1)}, u32[]{:S(2)}) %copy-start.4) | copy-done | bytes 3145752
  38.4 17.5 %layer.1 = (bf16[192,8192]{1,0:T(8,128)(2,1)}, f32[256,128,128]{2,1,0:T(8,128)}) custom-call(s32[1,64]{1,0:T(1,128)S(1)} %get-tuple-element.8.blocks, s32[1,256]{1,0:T(1,128)S(1)} %get-tuple-element.9.tiles, s32[1,256]{1,0:T(1,128)S(1)} %get-tuple-element.10.places, bf16[192,8192]{1,0:T(8,128)(2,1)S(1)} %copy-done.3, bf16[192,8192]{1,0:T(8,128)(2,1)S(1)} %copy-done.4, ...), custom_call_target="tpu_custom_call" | custom-call | flops 4831838208 | bytes 34603008 | tf_op jit(solution)/shard_map/layer/pallas_call | solution.py:128
  55.9 74.6 %reduce_terms.1 = bf16[8,2,4,1,128,128]{5,4,3,2,1,0:T(8,128)(2,1)S(1)} custom-call(f32[2,8,2,8,128,128]{5,4,3,2,1,0:T(8,128)} %bitcast.8), custom_call_target="tpu_custom_call" | custom-call | tf_op jit(solution)/shard_map/reduce_terms/pallas_call | solution.py:567
  130.5 2.7 %bitcast_convert_fusion = f32[64,128,128]{2,1,0:T(8,128)} fusion(bf16[8,2,4,1,128,128]{5,4,3,2,1,0:T(8,128)(2,1)S(1)} %reduce_terms.1), kind=kLoop, calls=%fused_computation | loop fusion | flops 1048576 | bytes 6291456 | tf_op jit(solution)/shard_map/convert_element_type | solution.py:620
Async XLA Ops:
  0.6 1.6 %copy-start = (bf16[64,128,128]{2,1,0:T(8,128)(2,1)S(1)}, bf16[64,128,128]{2,1,0:T(8,128)(2,1)}, u32[]{:S(2)}) copy-start(bf16[64,128,128]{2,1,0:T(8,128)(2,1)} %mine.1) | copy-start | bytes 6291460
  2.2 0.7 copy-start.1
  2.9 0.7 copy-start.2
  34.7 1.9 %copy-start.3 = (bf16[192,8192]{1,0:T(8,128)(2,1)S(1)}, bf16[192,8192]{1,0:T(8,128)(2,1)}, u32[]{:S(2)}) copy-start(bf16[192,8192]{1,0:T(8,128)(2,1)} %features.1) | copy-start | bytes 9437188
  36.5 1.9 %copy-start.4 = (bf16[192,8192]{1,0:T(8,128)(2,1)S(1)}, bf16[192,8192]{1,0:T(8,128)(2,1)}, u32[]{:S(2)}) copy-start(bf16[192,8192]{1,0:T(8,128)(2,1)} %grads.1) | copy-start | bytes 9437188

commit v9 on v8

--- a/solution.py
+++ b/solution.py
@@ -200,8 +200,8 @@
 
 
 def gather_kernel(
-    place, nw, pieces, find, mine, row, column, whole, blocks, order, places,
-    own_sem, xs, xr, ys, yr, zs, zr, ds, dr, cs, cr, ws, wr
+    place, nw, pieces, find, mine, row, column, features, grads,
+    whole, blocks, order, places, features_here, grads_here, rows_sem, own_sem, xs, xr, ys, yr, zs, zr, ds, dr, cs, cr, ws, wr
 ):
     me = place.locate()
     nx, ny = me.nx, me.ny
@@ -212,6 +212,10 @@
     other = me.at(c=1 - me.c)
     xp, yp = me.x_peers(), me.y_peers()
     zp = me.at(z=me.z + 1 - 2 * w) if nw == 2 else None
+    loads = [
+        pltpu.make_async_copy(features, features_here, rows_sem.at[0]),
+        pltpu.make_async_copy(grads, grads_here, rows_sem.at[1]),
+    ]
     meet(xp + yp + [other] + ([zp] if nw == 2 else []))
     run = ny * nw * q
     started = []
@@ -303,6 +307,8 @@
     for p in range(min(WINDOW, pieces)):
         for k in range(1, nx):
             x_copy(p, k, me.x).start()
+    for load in loads:
+        load.start()
     blocks[...], order[...], places[...] = find(row[...], column[...])
     stages = [land_x, land_yz] + ([land_last] if nw == 2 else [])
     for t in range(pieces + len(stages) - 1):
@@ -319,11 +325,13 @@
                 for v in range(nw):
                     u = w if v == 0 else 1 - w
                     in_chip(k, j, v, p, span(x, y, u, p, 1 - me.c)).wait_recv()
+    for load in loads:
+        load.wait()
     for copy in started:
         copy.wait_send()
 
 
-def gather_tiles(mine, tile_row, tile_column, nblocks, run, place):
+def gather_tiles(mine, tile_row, tile_column, features, grad_out, nblocks, run, place):
     tiles, side, _ = mine.shape
     nx, ny = place.nx, place.ny
     nw = 2 if place.nz % 2 == 0 and tiles % (2 * ny) == 0 else 1
@@ -335,15 +343,17 @@
     dma = pltpu.SemaphoreType.DMA
     return pl.pallas_call(
         functools.partial(gather_kernel, place, nw, pieces, find),
-        in_specs=[vmem] * 3,
-        out_specs=[vmem] * 4,
+        in_specs=[vmem] * 3 + [pl.BlockSpec(memory_space=pl.ANY)] * 2,
+        out_specs=[vmem] * 6,
         out_shape=[
             jax.ShapeDtypeStruct((total, side, side), mine.dtype),
             jax.ShapeDtypeStruct((1, nblocks), jnp.int32),
             jax.ShapeDtypeStruct((1, total), jnp.int32),
             jax.ShapeDtypeStruct((1, total), jnp.int32),
+            jax.ShapeDtypeStruct(features.shape, features.dtype),
+            jax.ShapeDtypeStruct(grad_out.shape, grad_out.dtype),
         ],
-        scratch_shapes=[dma((pieces,))]
+        scratch_shapes=[dma((2,)), dma((pieces,))]
         + [dma((nx - 1, pieces))] * 2
         + [dma((nx - 1, ny - 1, pieces))] * 2
         + [dma((nx - 1, pieces))] * 2
@@ -354,7 +364,7 @@
             collective_id=1, has_side_effects=True, vmem_limit_bytes=24 * 2**20
         ),
         name="gather_tiles",
-    )(mine, tile_row.reshape(1, total), tile_column.reshape(1, total))
+    )(mine, tile_row.reshape(1, total), tile_column.reshape(1, total), features, grad_out)
 
 
 def reduce_kernel(
@@ -611,8 +621,8 @@
     nx, n = place.nx, place.ny * place.nz
     pieces = max(count for count in (1, 2, 4, 8) if tiles_here % (n * count) == 0)
     n = tiles_here // pieces
-    whole, blocks, tiles, places = gather_tiles(
-        weight_tiles, tile_row, tile_column, nblocks, n, place
+    whole, blocks, tiles, places, features, grad_out = gather_tiles(
+        weight_tiles, tile_row, tile_column, features, grad_out, nblocks, n, place
     )
     grad_features, partial = layer(features, grad_out, whole, blocks, tiles, places)
     terms = partial.reshape(2, pieces, nx, n, side, side)

time: 134 us -> 133 us (level)
  no operation moved by 1% of the time
where the time goes in v9:
time: 133 us
  Pallas kernels  123 us (92%)
  local copies, waits for them, and re-layouts  6.72 us (5%)
  other arithmetic  2.68 us (2%)
    pallas_call x1, Pallas kernels, reduce_terms(): pl.pallas_call(functools.partial(reduce_kernel, place, pieces, q), in_spe...  74.6 us
    pallas_call x1, Pallas kernels, gather_tiles(): pl.pallas_call(functools.partial(gather_kernel, place, nw, pieces, find),...  31.1 us
    pallas_call x1, Pallas kernels, layer(): pl.pallas_call(functools.partial(layer_kernel, steps), in_specs=[smem] *...  17.5 us
    unnamed x10, local copies, waits for them, and re-layouts  6.72 us
    convert_element_type x1, other arithmetic, on_device(): tile_update.reshape(tiles_here, side, side).astype(jnp.float32)  2.68 us

profile of v9, /device:TPU:0, one launch (start us, length us, event | category | flops | bytes accessed | tf_op | source)
XLA Modules:
  0.0 133.2 jit_solution(13001808073043478877)
XLA Ops:
  0.6 0.0 copy-start
  0.6 1.9 %copy-done = bf16[192,8192]{1,0:T(8,128)(2,1)S(1)} copy-done((bf16[192,8192]{1,0:T(8,128)(2,1)S(1)}, bf16[192,8192]{1,0:T(8,128)(2,1)}, u32[]{:S(2)}) %copy-start) | copy-done | bytes 3145752
  2.5 0.0 copy-start.1
  2.5 1.9 %copy-done.1 = bf16[192,8192]{1,0:T(8,128)(2,1)S(1)} copy-done((bf16[192,8192]{1,0:T(8,128)(2,1)S(1)}, bf16[192,8192]{1,0:T(8,128)(2,1)}, u32[]{:S(2)}) %copy-start.1) | copy-done | bytes 3145752
  4.4 0.0 copy-start.2
  4.4 1.6 %copy-done.2 = bf16[64,128,128]{2,1,0:T(8,128)(2,1)S(1)} copy-done((bf16[64,128,128]{2,1,0:T(8,128)(2,1)S(1)}, bf16[64,128,128]{2,1,0:T(8,128)(2,1)}, u32[]{:S(2)}) %copy-start.2) | copy-done | bytes 2097176
  6.0 0.0 copy-start.3
  6.0 0.7 copy-done.3
  6.7 0.0 copy-start.4
  6.7 0.7 copy-done.4
  7.4 31.1 %gather_tiles.1 = (bf16[256,128,128]{2,1,0:T(8,128)(2,1)S(1)}, s32[1,64]{1,0:T(1,128)S(1)}, s32[1,256]{1,0:T(1,128)S(1)}, s32[1,256]{1,0:T(1,128)S(1)}, bf16[192...) custom-call(bf16[64,128,128]{2,1,0:T(8,128)(2,1)S(1)} %copy-done.2, s32[1,256]{1,0:T(1,128)S(1)} %bitcast.6, ...), custom_call_target="tpu_custom_call" | custom-call | tf_op jit(solution)/shard_map/gather_tiles/pallas_call | solution.py:344
  38.4 17.5 %layer.1 = (bf16[192,8192]{1,0:T(8,128)(2,1)}, f32[256,128,128]{2,1,0:T(8,128)}) custom-call(s32[1,64]{1,0:T(1,128)S(1)} %get-tuple-element.10.blocks, s32[1,256]{1,0:T(1,128)S(1)} %get-tuple-element.11.tiles, s32[1,256]{1,0:T(1,128)S(1)} %get-tuple-element.12.places, bf16[192,8192]{1,0:T(8,128)(2,1)S(1)} %get-tuple-element.13.features, ...), custom_call_target="tpu_custom_call" | custom-call | flops 4831838208 | bytes 34603008 | tf_op jit(solution)/shard_map/layer/pallas_call | solution.py:128
  55.9 74.6 %reduce_terms.1 = bf16[8,2,4,1,128,128]{5,4,3,2,1,0:T(8,128)(2,1)S(1)} custom-call(f32[2,8,2,8,128,128]{5,4,3,2,1,0:T(8,128)} %bitcast.8), custom_call_target="tpu_custom_call" | custom-call | tf_op jit(solution)/shard_map/reduce_terms/pallas_call | solution.py:577
  130.5 2.7 %bitcast_convert_fusion = f32[64,128,128]{2,1,0:T(8,128)} fusion(bf16[8,2,4,1,128,128]{5,4,3,2,1,0:T(8,128)(2,1)S(1)} %reduce_terms.1), kind=kLoop, calls=%fused_computation | loop fusion | flops 1048576 | bytes 6291456 | tf_op jit(solution)/shard_map/convert_element_type | solution.py:630
Async XLA Ops:
  0.6 1.9 %copy-start = (bf16[192,8192]{1,0:T(8,128)(2,1)S(1)}, bf16[192,8192]{1,0:T(8,128)(2,1)}, u32[]{:S(2)}) copy-start(bf16[192,8192]{1,0:T(8,128)(2,1)} %features.1) | copy-start | bytes 9437188
  2.5 1.9 %copy-start.1 = (bf16[192,8192]{1,0:T(8,128)(2,1)S(1)}, bf16[192,8192]{1,0:T(8,128)(2,1)}, u32[]{:S(2)}) copy-start(bf16[192,8192]{1,0:T(8,128)(2,1)} %grads.1) | copy-start | bytes 9437188
  4.4 1.6 %copy-start.2 = (bf16[64,128,128]{2,1,0:T(8,128)(2,1)S(1)}, bf16[64,128,128]{2,1,0:T(8,128)(2,1)}, u32[]{:S(2)}) copy-start(bf16[64,128,128]{2,1,0:T(8,128)(2,1)} %mine.1) | copy-start | bytes 6291460
  6.0 0.7 copy-start.3
  6.7 0.7 copy-start.4
